TPU v7x, 512 devices: a whole 4x8x8 slice. The times are simulated.
512 devices in a mesh: shard: 64 (over x, z, core), grp: 8 (over y).
Axes of the slice: x: 4, y: 8, z: 8, core: 2. Of those that a mesh axis runs over, the one named last changes fastest.
Arguments:
- emb_table: bfloat16 [131072, 192], P('shard'), may hold values from -3 to 3
- touched: int32 [64, 8, 64, 64], P('shard', 'grp'), may hold values from -1 to 2047, as said below
- bag_slots: int32 [1024, 384, 4], P('shard', 'grp'), may hold values from -1 to 4095, as said below
- feat_of_slot: int32 [8, 48], P('grp'), may hold values from -1 to 255, as said below
- lcb_weight: bfloat16 [256, 256], replicated, may hold values from -0.375 to 0.375
- proj_weight: bfloat16 [256, 64], replicated, may hold values from -0.375 to 0.375
- fm_weight: bfloat16 [64, 192], replicated, may hold values from -0.0546875 to 0.0546875
- ln_gain: float32 [192], replicated, may hold values from 0.5 to 1.5
- cotangent: bfloat16 [1024, 256, 192], P(('shard', 'grp')), may hold values from -6 to 6
Outputs:
- interacted: bfloat16 [1024, 256, 192], P(('shard', 'grp'))
- table_grad: float32 [131072, 192], P(('shard', 'grp'))
- lcb_grad: float32 [256, 256], replicated
- proj_grad: float32 [256, 64], replicated
- fm_grad: float32 [64, 192], replicated
Inputs may be any that keep to these rules, and one draw needn't show every extreme that they name: `touched`: for each device of the batch and each owner, a list of 64 slots: one or more distinct local rows, then -1 to the end of the list. In every draw one owner's list is full from every device of the batch. `bag_slots`: each entry is -1 or a slot o * 64 + k of the device's own lists (its block of samples and its group) whose row in touched is not -1. The bag of a slot that feat_of_slot marks -1 is all -1; the bag of a live slot has one entry or more, its -1 entries after the others. `feat_of_slot`: each feature of 0 to 255 is held by exactly one slot over all groups; in each group the live slots come first, then -1.
All inputs are finite; a program needn't handle non-finite values.
Results may differ from a plain program's by a relative error of at most 0.013.
Values may be sent and summed in bfloat16 or wider, within the bound.
A program may use at most 64 MiB of HBM per device.

v0:
```python
import jax
import jax.numpy as jnp
from jax import lax
from jax.sharding import PartitionSpec as P

norm_epsilon = 1e-05


def layer_pass(embedded, lcb_weight, proj_weight, fm_weight, ln_gain, upstream):
    wide_out = jnp.float32
    linear_part = jnp.einsum("bfd,fg->bgd", embedded, lcb_weight, preferred_element_type=wide_out)
    low_rank = jnp.einsum(
        "bfd,fr->bdr", embedded, proj_weight, preferred_element_type=wide_out
    ).astype(jnp.bfloat16)
    crossed = jnp.einsum(
        "bfd,bdr->bfr", embedded, low_rank, preferred_element_type=wide_out
    ).astype(jnp.bfloat16)
    fm_part = jnp.einsum("bfr,rd->bfd", crossed, fm_weight, preferred_element_type=wide_out)
    summed = embedded.astype(jnp.float32) + linear_part + fm_part
    center = summed - jnp.mean(summed, axis=-1, keepdims=True)
    inv_std = lax.rsqrt(jnp.mean(center * center, axis=-1, keepdims=True) + norm_epsilon)
    normed = center * inv_std
    result = (normed * ln_gain).astype(jnp.bfloat16)
    scaled = upstream.astype(jnp.float32) * ln_gain
    grad_sum = inv_std * (
        scaled
        - jnp.mean(scaled, axis=-1, keepdims=True)
        - normed * jnp.mean(scaled * normed, axis=-1, keepdims=True)
    )
    grad_low = grad_sum.astype(jnp.bfloat16)
    grad_cross = jnp.einsum(
        "bfd,rd->bfr", grad_low, fm_weight, preferred_element_type=wide_out
    ).astype(jnp.bfloat16)
    fm_grad = jnp.einsum("bfr,bfd->rd", crossed, grad_low, preferred_element_type=wide_out)
    grad_proj = jnp.einsum(
        "bfd,bfr->bdr", embedded, grad_cross, preferred_element_type=wide_out
    ).astype(jnp.bfloat16)
    proj_grad = jnp.einsum("bfd,bdr->fr", embedded, grad_proj, preferred_element_type=wide_out)
    lcb_grad = jnp.einsum("bfd,bgd->fg", embedded, grad_low, preferred_element_type=wide_out)
    grad_in = (
        grad_sum
        + jnp.einsum("fg,bgd->bfd", lcb_weight, grad_low, preferred_element_type=wide_out)
        + jnp.einsum("bfr,bdr->bfd", grad_cross, low_rank, preferred_element_type=wide_out)
        + jnp.einsum("fr,bdr->bfd", proj_weight, grad_proj, preferred_element_type=wide_out)
    )
    return (result, grad_in.astype(jnp.bfloat16), lcb_grad, proj_grad, fm_grad)


def shards(
    emb_table,
    touched,
    bag_slots,
    feat_of_slot,
    lcb_weight,
    proj_weight,
    fm_weight,
    ln_gain,
    cotangent,
):
    owners = lax.axis_size("shard")
    wanted = touched[0, 0]
    capacity = wanted.shape[1]
    feat_width = emb_table.shape[1]
    table_rows = emb_table.shape[0]
    requested = lax.all_to_all(wanted, "shard", split_axis=0, concat_axis=0, tiled=True)
    served = emb_table[jnp.maximum(requested, 0)]
    fetched = lax.all_to_all(served, "shard", split_axis=0, concat_axis=0, tiled=True)
    buffer_rows = fetched.reshape(owners * capacity, feat_width)
    bag_count = bag_slots.shape[2]
    pooled = jnp.zeros(bag_slots.shape[:2] + (feat_width,), jnp.float32)
    for bag_pos in range(bag_count):
        bag_entry = bag_slots[:, :, bag_pos]
        picked = buffer_rows[jnp.maximum(bag_entry, 0)]
        pooled = pooled + jnp.where((bag_entry >= 0)[..., None], picked.astype(jnp.float32), 0.0)
    pooled = pooled.astype(jnp.bfloat16)
    arrived = lax.all_to_all(pooled, "grp", split_axis=0, concat_axis=1, tiled=True)
    flat_feats = lax.all_gather(feat_of_slot, "grp", axis=0, tiled=True).reshape(-1)
    features = lcb_weight.shape[0]
    slot_total = flat_feats.shape[0]
    target = jnp.where(flat_feats >= 0, flat_feats, features)
    slot_of_feature = (
        jnp.zeros((features,), jnp.int32)
        .at[target]
        .set(jnp.arange(slot_total, dtype=jnp.int32), mode="drop")
    )
    embedded = arrived[:, slot_of_feature, :]
    result, grad_in, lcb_part, proj_part, fm_part = layer_pass(
        embedded, lcb_weight, proj_weight, fm_weight, ln_gain, cotangent
    )
    lcb_grad, proj_grad, fm_grad = lax.psum((lcb_part, proj_part, fm_part), ("shard", "grp"))
    live_slot = (flat_feats >= 0)[None, :, None]
    slot_grad_in = jnp.where(
        live_slot, grad_in[:, jnp.maximum(flat_feats, 0), :], jnp.zeros((), jnp.bfloat16)
    )
    returned = lax.all_to_all(slot_grad_in, "grp", split_axis=1, concat_axis=0, tiled=True)
    returned_wide = returned.astype(jnp.float32)
    slot_grad = jnp.zeros((owners * capacity, feat_width), jnp.float32)
    for bag_pos in range(bag_count):
        bag_entry = bag_slots[:, :, bag_pos]
        slot_grad = slot_grad.at[jnp.maximum(bag_entry, 0)].add(
            jnp.where((bag_entry >= 0)[..., None], returned_wide, 0.0)
        )
    row_index = jnp.maximum(requested, 0).reshape(-1)
    incoming = lax.all_to_all(
        slot_grad.reshape(owners, capacity, feat_width).astype(jnp.bfloat16),
        "shard",
        split_axis=0,
        concat_axis=0,
        tiled=True,
    ).astype(jnp.float32)
    dense_grad = (
        jnp.zeros((table_rows, feat_width), jnp.float32)
        .at[row_index]
        .add(incoming.reshape(-1, feat_width))
    )
    table_grad = lax.psum_scatter(
        dense_grad.astype(jnp.bfloat16), "grp", scatter_dimension=0, tiled=True
    ).astype(jnp.float32)
    return (result, table_grad, lcb_grad, proj_grad, fm_grad)


def solution(mesh):
    placed = (
        P("shard", None),
        P("shard", "grp", None, None),
        P("shard", "grp", None),
        P("grp", None),
        P(),
        P(),
        P(),
        P(),
        P(("shard", "grp"), None, None),
    )
    return jax.shard_map(
        shards,
        mesh=mesh,
        in_specs=placed,
        out_specs=(P(("shard", "grp"), None, None), P(("shard", "grp"), None), P(), P(), P()),
        check_vma=False,
    )
```

profile of v0, /device:TPU:1, one launch (start us, length us, event | category | flops | bytes accessed | tf_op | source)
XLA Modules:
  0.0 575.8 jit_solution(6774591251504211974)
XLA Ops:
  8.0 15.0 %all-to-all-start = ((s32[64,1,64]{2,1,0:T(1,128)}), s32[64,1,64]{2,1,0:T(1,128)S(1)}, u32[]{:S(2)}, u32[]{:S(2)}) async-start(s32[64,1,64]{2,1,0:T(1,128)} %bitcast.142), calls=%async_computation | async-start | bytes 65536 | tf_op jit(solution)/shard_map/all_to_all | solution.py:65
  23.0 1.4 copy.53
  24.4 7.8 %all-to-all-done = s32[64,1,64]{2,1,0:T(1,128)S(1)} async-done(((s32[64,1,64]{2,1,0:T(1,128)}), s32[64,1,64]{2,1,0:T(1,128)S(1)}, u32[]{:S(2)}, u32[]{:S(2)}) %all-to-all-start) | async-done | bytes 16416 | tf_op jit(solution)/shard_map/all_to_all | solution.py:65
  32.2 0.1 maximum_reduce_fusion
  32.3 0.1 reshape.133
  32.4 16.9 %gather_fusion = bf16[4096,192]{1,0:T(8,128)(2,1)} fusion(bf16[2048,192]{1,0:T(8,128)(2,1)S(1)} %copy.53, s32[4096]{0:T(1024)S(1)} %broadcast_clamp_fusion), kind=kCustom, calls=%fused_computation | custom fusion | bytes 3162112 | tf_op jit(solution)/shard_map/gather | solution.py:66
  49.3 4.9 all-to-all-start.1
  54.3 14.1 %all-gather = s32[8,1,48]{2,1,0:T(1,128)S(1)} all-gather(s32[1,1,48]{2,1,0:T(1,128)S(1)} %bitcast.143), channel_id=1, replica_groups=mesh['shard'=64,'grp'=8] {'grp'}, dimensions={0}, use_global_device_ids=true | all-gather | bytes 1728 | tf_op jit(solution)/shard_map/all_gather | solution.py:77
  68.3 0.5 broadcast.197
  68.8 0.7 reduce.13
  69.5 0.1 reshape.124
  69.6 0.1 ge.46
  69.7 0.1 reshape.157
  69.8 0.1 reshape.165
  69.9 0.1 reshape.141
  70.0 0.1 reshape.149
  70.1 35.5 %all-to-all-done.1 = bf16[64,64,192]{2,1,0:T(8,128)(2,1)S(1)} async-done(((bf16[64,64,192]{2,1,0:T(8,128)(2,1)}), bf16[64,64,192]{2,1,0:T(8,128)(2,1)S(1)}, u32[]{:S(2)}, u32[]{:S(2)}) %all-to-all-start.1) | async-done | bytes 1572896 | tf_op jit(solution)/shard_map/all_to_all | solution.py:67
  105.6 2.6 gather_fusion.4
  108.3 2.7 gather_fusion.3
  110.9 2.7 gather_fusion.2
  113.6 3.3 gather_fusion.1
  116.9 2.2 fusion.10
  119.1 6.8 %all-to-all-start.2 = ((bf16[16,48,192]{2,1,0:T(8,128)(2,1)}), bf16[16,48,192]{2,1,0:T(8,128)(2,1)S(1)}, u32[]{:S(2)}, u32[]{:S(2)}) async-start(bf16[16,48,192]{2,1,0:T(8,128)(2,1)} %fusion.10), calls=%async_computation.2 | async-start | bytes 786432 | tf_op jit(solution)/shard_map/all_to_all | solution.py:76
  126.0 3.1 scatter_custom_fusion
  129.1 11.9 %all-to-all-done.2 = bf16[16,48,192]{2,1,0:T(8,128)(2,1)S(1)} async-done(((bf16[16,48,192]{2,1,0:T(8,128)(2,1)}), bf16[16,48,192]{2,1,0:T(8,128)(2,1)S(1)}, u32[]{:S(2)}, u32[]{:S(2)}) %all-to-all-start.2) | async-done | bytes 294944 | tf_op jit(solution)/shard_map/all_to_all | solution.py:76
  141.1 0.4 copy.58
  141.5 1.2 gather_fusion.5
  142.8 0.2 copy.59
  142.9 0.2 convolution_convert_fusion.3
  143.1 0.2 convolution_convert_fusion.1
  143.3 0.2 fusion.6
  143.5 0.3 fusion.32
  143.8 0.1 multiply_reduce_fusion.1
  143.9 0.1 fusion.13
  144.1 0.8 fusion.23
  144.9 0.2 fusion.5
  145.2 0.2 convolution_convert_fusion
  145.3 0.2 convolution_convert_fusion.2
  145.5 0.3 convolution_add_fusion
  145.8 0.2 fusion.7
  146.0 0.2 copy.60
  146.2 2.5 gather_fusion.6
  148.8 1.3 fusion.14
  150.1 16.7 %all_to_all.46 = bf16[2,384,192]{2,0,1:T(2,128)(2,1)S(1)} all-to-all(bf16[2,384,192]{2,0,1:T(2,128)(2,1)S(1)} %fusion.14), channel_id=1, replica_groups=mesh['shard'=64,'grp'=8] {'grp'}, dimensions={1} | all-to-all | bytes 589824 | tf_op jit(solution)/shard_map/all_to_all | solution.py:95
  166.8 0.8 copy.61
  167.5 0.2 copy.62
  167.7 0.1 copy.63
  167.8 1.4 bitcast_select_fusion
  169.1 8.5 %scatter_custom_fusion.1 = f32[4096,192]{1,0:T(8,128)} fusion(s32[768]{0:T(1024)S(1)} %reshape.141, f32[768,192]{1,0:T(8,128)} %bitcast.133, f32[]{:T(128)} %constant.12.clone.1), kind=kCustom, calls=%fused_computation.15 | custom fusion | flops 147456 | bytes 3146240 | tf_op jit(solution)/shard_map/scatter-add | solution.py:100
  177.6 10.3 %scatter_fusion = f32[4096,192]{1,0:T(8,128)} fusion(f32[4096,192]{1,0:T(8,128)} %scatter_custom_fusion.1, s32[768]{0:T(1024)S(1)} %reshape.149, f32[768,192]{1,0:T(8,128)S(1)} %bitcast.126), kind=kCustom, calls=%fused_computation.9 | custom fusion | flops 147456 | bytes 1772544 | tf_op jit(solution)/shard_map/scatter-add | solution.py:100
  187.9 10.3 %scatter_fusion.1 = f32[4096,192]{1,0:T(8,128)} fusion(f32[4096,192]{1,0:T(8,128)} %scatter_fusion, s32[768]{0:T(1024)S(1)} %reshape.157, f32[768,192]{1,0:T(8,128)S(1)} %bitcast.125), kind=kCustom, calls=%fused_computation.10 | custom fusion | flops 147456 | bytes 1772544 | tf_op jit(solution)/shard_map/scatter-add | solution.py:100
  198.2 10.5 %scatter_fusion.2 = f32[4096,192]{1,0:T(8,128)} fusion(f32[4096,192]{1,0:T(8,128)} %scatter_fusion.1, s32[768]{0:T(1024)S(1)} %reshape.165, f32[768,192]{1,0:T(8,128)S(1)} %bitcast.124), kind=kCustom, calls=%fused_computation.11 | custom fusion | flops 147456 | bytes 1772544 | tf_op jit(solution)/shard_map/scatter-add | solution.py:100
  208.8 2.4 convert_element_type.85
  211.2 57.9 %all_to_all.47 = bf16[64,64,192]{2,1,0:T(8,128)(2,1)S(1)} all-to-all(bf16[64,64,192]{2,1,0:T(8,128)(2,1)S(1)} %bitcast.121), channel_id=1, replica_groups=mesh['shard'=64,'grp'=8] {'shard'}, dimensions={0} | all-to-all | bytes 3145728 | tf_op jit(solution)/shard_map/all_to_all | solution.py:104
  269.1 26.3 %scatter_custom_fusion.5 = f32[2048,192]{1,0:T(8,128)} fusion(s32[4096]{0:T(1024)S(1)} %reshape.133, bf16[4096,192]{1,0:T(8,128)(2,1)S(1)} %bitcast.122, f32[]{:T(128)} %constant.12.clone.1), kind=kCustom, calls=%fused_computation.13 | custom fusion | flops 1572864 | bytes 3670020 | tf_op jit(solution)/shard_map/scatter-add | solution.py:114
  295.4 2.7 convert_element_type.87
  298.2 0.8 convolution_bitcast_fusion.4
  299.0 1.0 convolution_bitcast_fusion.3
  300.0 0.2 convolution_bitcast_fusion.5
  300.2 96.5 %psum.23 = f32[64,192]{1,0:T(8,128)} all-reduce(f32[64,192]{1,0:T(8,128)S(1)} %convolution_bitcast_fusion.5), channel_id=1, replica_groups=mesh['shard'=64,'grp'=8] {'shard','grp'}, use_global_device_ids=true, to_apply=%region_13.14 | all-reduce | flops 12288 | bytes 98304 | tf_op jit(solution)/shard_map/psum | solution.py:90
  396.7 1.7 copy.64
  398.3 166.9 %all-reduce.3.cloned.1.call-done = (f32[256,256]{1,0:T(8,128)}, f32[256,64]{0,1:T(8,128)}) async-done(((f32[256,256]{1,0:T(8,128)}, f32[256,64]{0,1:T(8,128)}), (f32[256,256]{1,0:T(8,128)}, f32[256,64]{0,1:T(8,128)})) %all-reduce.3.cloned.1.call-update) | async-done | bytes 327696 | tf_op jit(solution)/shard_map/psum | solution.py:90
  565.2 1.7 copy.74
  566.9 1.5 copy.75
  (42 shorter events, 0.3 us)
Async XLA Ops:
  8.0 135.3 %copy-start = (bf16[256,256]{1,0:T(8,128)(2,1)S(1)}, bf16[256,256]{1,0:T(8,128)(2,1)}, u32[]{:S(2)}) copy-start(bf16[256,256]{1,0:T(8,128)(2,1)} %param.13) | copy-start | bytes 393220
  8.0 24.2 %all-to-all-start = ((s32[64,1,64]{2,1,0:T(1,128)}), s32[64,1,64]{2,1,0:T(1,128)S(1)}, u32[]{:S(2)}, u32[]{:S(2)}) async-start(s32[64,1,64]{2,1,0:T(1,128)} %bitcast.142), calls=%async_computation | async-start | bytes 65536 | tf_op jit(solution)/shard_map/all_to_all | solution.py:65
  49.3 4.9 copy-start.6
  49.3 20.4 %copy-start.4 = (s32[16,48,4]{1,2,0:T(4,128)S(1)}, s32[16,48,4]{1,2,0:T(4,128)}, u32[]{:S(2)}) copy-start(s32[16,48,4]{1,2,0:T(4,128)} %param.11) | copy-start | bytes 36868
  49.3 56.3 %all-to-all-start.1 = ((bf16[64,64,192]{2,1,0:T(8,128)(2,1)}), bf16[64,64,192]{2,1,0:T(8,128)(2,1)S(1)}, u32[]{:S(2)}, u32[]{:S(2)}) async-start(bf16[64,64,192]{2,1,0:T(8,128)(2,1)} %bitcast.120), calls=%async_computation.1 | async-start | bytes 4194304 | tf_op jit(solution)/shard_map/all_to_all | solution.py:67
  113.6 29.3 %copy-start.3 = (bf16[256,64]{0,1:T(8,128)(2,1)S(1)}, bf16[256,64]{0,1:T(8,128)(2,1)}, u32[]{:S(2)}) copy-start(bf16[256,64]{0,1:T(8,128)(2,1)} %param.14) | copy-start | bytes 98308
  116.9 26.6 %copy-start.2 = (bf16[64,192]{1,0:T(8,128)(2,1)S(1)}, bf16[64,192]{1,0:T(8,128)(2,1)}, u32[]{:S(2)}) copy-start(bf16[64,192]{1,0:T(8,128)(2,1)} %param.15) | copy-start | bytes 73732
  116.9 27.0 %copy-start.1 = (bf16[2,256,192]{1,2,0:T(8,128)(2,1)S(1)}, bf16[2,256,192]{1,2,0:T(8,128)(2,1)}, u32[]{:S(2)}) copy-start(bf16[2,256,192]{1,2,0:T(8,128)(2,1)} %param.17) | copy-start | bytes 589828
  116.9 27.0 %copy-start.5 = (f32[192]{0:T(256)S(1)}, f32[192]{0:T(256)}, u32[]{:S(2)}) copy-start(f32[192]{0:T(256)} %param.16) | copy-start | bytes 2308
  119.1 22.0 %all-to-all-start.2 = ((bf16[16,48,192]{2,1,0:T(8,128)(2,1)}), bf16[16,48,192]{2,1,0:T(8,128)(2,1)S(1)}, u32[]{:S(2)}, u32[]{:S(2)}) async-start(bf16[16,48,192]{2,1,0:T(8,128)(2,1)} %fusion.10), calls=%async_computation.2 | async-start | bytes 786432 | tf_op jit(solution)/shard_map/all_to_all | solution.py:76
  125.9 270.7 %reduce-scatter.2.cloned.1.call-start = ((), (), s32[]{:S(2)}) async-start(), calls=%async_computation.6 | async-start | bytes 1179648 | tf_op jit(solution)/shard_map/reduce_scatter | solution.py:116
  298.1 267.1 %all-reduce.3.cloned.1.call-start = ((), (), s32[]{:S(2)}) async-start(), calls=%async_computation.7 | async-start | bytes 655360 | tf_op jit(solution)/shard_map/psum | solution.py:90
Sparse Core Ops, SparseCore 0:
  298.2 28.1 reduce-scatter.1
Sparse Core Ops, SparseCore 1:
  304.1 261.0 all-reduce.2
where the time goes:
time: 577 us; the launch traced here: 576 us
  waiting for transfers between devices  222 us (38%)
  blocking collectives  185 us (32%)
  other arithmetic  77.9 us (14%)
  local copies, waits for them, and re-layouts  44.1 us (8%)
  starting transfers between devices  26.8 us (5%)
  between operations  15.9 us (3%)
    psum x1, waiting for transfers between devices, shards(): lax.psum((lcb_part, proj_part, fm_part), ('shard', 'grp'))  167 us
    psum x1, blocking collectives, shards(): lax.psum((lcb_part, proj_part, fm_part), ('shard', 'grp'))  96.5 us
    all_to_all x1, blocking collectives, shards(): lax.all_to_all(slot_grad.reshape(owners, capacity, feat_width).astype(jnp...  57.9 us
    scatter-add x4, other arithmetic, shards(): slot_grad.at[jnp.maximum(bag_entry, 0)]  39.6 us
    all_to_all x1, waiting for transfers between devices, shards(): lax.all_to_all(served, 'shard', split_axis=0, concat_axis=0, tiled=True)  35.5 us
    scatter-add x1, other arithmetic, shards(): dense_grad = jnp.zeros((table_rows, feat_width), jnp.float32).at[row_inde...  26.3 us
    gather x1, local copies, waits for them, and re-layouts, shards(): served = emb_table[jnp.maximum(requested, 0)]  16.9 us
    all_to_all x1, blocking collectives, shards(): lax.all_to_all(slot_grad_in, 'grp', split_axis=1, concat_axis=0, tiled=True)  16.7 us
  transfers between devices with their start and end apart: 5, of which 4 were waited for; matrix products, arithmetic and copies ran while one was open for 2% of the time, Pallas kernels for 0%

commit v1 on v0

v1 whole, which is shorter than its diff:
```python
import functools

import jax
import jax.numpy as jnp
from jax import lax
from jax.experimental import pallas as pl
from jax.experimental.pallas import tpu as pltpu
from jax.sharding import PartitionSpec as P

MESH = pl.DeviceIdType.MESH
norm_epsilon = 1e-05
LANES = 128
HALF = 64
BF = jnp.bfloat16
F32 = jnp.float32


def nn(a, b):
    return lax.dot_general(a, b, (((1,), (0,)), ((), ())), preferred_element_type=F32)


def nt(a, b):
    return lax.dot_general(a, b, (((1,), (1,)), ((), ())), preferred_element_type=F32)


def wait_all(ref, sem):
    pltpu.make_async_copy(ref, ref, sem).wait()


def pack_pair(x, low):
    m = x.shape[0] // 2
    turned = pltpu.roll(x, HALF, 1)
    even = jnp.where(low, x[:m], turned[m:])
    odd = jnp.where(low, turned[:m], x[m:])
    return even.astype(BF), odd.astype(BF)


def unpack_pair(even, odd, low):
    even, odd = even.astype(F32), odd.astype(F32)
    top = jnp.where(low, even, pltpu.roll(odd, HALF, 1))
    bottom = jnp.where(low, pltpu.roll(even, HALF, 1), odd)
    return jnp.concatenate([top, bottom], axis=0).astype(BF)


def kernel(
    X, Z, G,
    lists_ref, bag_ref, feat_ref, table_ref, lcb_ref, projt_ref, fm_ref, fmt_ref, gain_ref, cot_ref,
    inter_ref, tgrad_ref, lcbg_ref, projg_ref, fmg_ref,
    lists_in, feat_in, oh, mt, sbuf, rbuf, wide, pooled, esend, erecv, pm, gsend, grecv, gt,
    hsend, hrecv, tacc, jsend, jrecv, w, k1, a2, k2, b3, k3, c4, k4, d5, k5, total,
    send_sem, list_sem, row_sem, grad_sem, grp_sem,
):
    S = X * Z * 2
    groups = X * 2
    me_s = lax.axis_index("shard")
    me_g = lax.axis_index("grp")
    core = lax.rem(me_s, 2)
    me_z = lax.rem(lax.div(me_s, 2), Z)
    me_x = lax.div(me_s, 2 * Z)
    slot_rows = HALF * Z
    rows = table_ref.shape[1]
    width = table_ref.shape[0]
    features = lcb_ref.shape[0]
    bags = bag_ref.shape[0]
    bag_lanes = bag_ref.shape[1]

    def peer(q, back):
        i = lax.rem(q, Z)
        j = lax.div(q, Z)
        dc = lax.rem(j, 2)
        dx = lax.rem(lax.div(j, 2) + i, X)
        if back:
            x, z = lax.rem(me_x + X - dx, X), lax.rem(me_z + Z - i, Z)
        else:
            x, z = lax.rem(me_x + dx, X), lax.rem(me_z + i, Z)
        return (x * Z + z) * 2 + lax.rem(core + dc, 2)

    def send(src, dst, ssem, rsem, **where):
        pltpu.make_async_remote_copy(
            src_ref=src, dst_ref=dst, send_sem=ssem, recv_sem=rsem,
            device_id=where, device_id_type=MESH,
        ).start()

    def group_back(k):
        return lax.rem(me_g + G - k, G)

    def group_ahead(k):
        return lax.rem(me_g + k, G)

    barrier = pltpu.get_barrier_semaphore()

    def greet_shard(q, carry):
        pl.semaphore_signal(barrier, inc=1, device_id={"shard": peer(q, False)}, device_id_type=MESH)
        return carry

    def greet_group(k, carry):
        pl.semaphore_signal(barrier, inc=1, device_id={"grp": group_ahead(k)}, device_id_type=MESH)
        return carry

    lax.fori_loop(1, S, greet_shard, 0)
    lax.fori_loop(1, G, greet_group, 0)
    pl.semaphore_wait(barrier, S - 1 + G - 1)

    def send_list(q, carry):
        to = peer(q, True)
        send(lists_ref.at[to], lists_in.at[q], send_sem.at[0], list_sem.at[lax.div(q, Z)], shard=to)
        return carry

    lax.fori_loop(1, S, send_list, 0)
    lists_in[0] = lists_ref[me_s]

    def send_feat(k, carry):
        send(feat_ref, feat_in.at[k], send_sem.at[1], grp_sem.at[0], grp=group_back(k))
        return carry

    lax.fori_loop(1, G, send_feat, 0)
    feat_in[0] = feat_ref[...]

    low1 = lax.broadcasted_iota(jnp.int32, (1, LANES), 1) < HALF
    low = lax.broadcasted_iota(jnp.int32, (width // 2, LANES), 1) < HALF

    row_line = lax.broadcasted_iota(jnp.int32, (256, LANES), 0)

    def serve(j, first):
        if first:
            wait_all(lists_in.at[pl.ds(1, Z - 1)], list_sem.at[j])
        else:
            wait_all(lists_in.at[pl.ds(j * Z, Z)], list_sem.at[j])
        for p in range(Z // 2):
            want = jnp.where(low1, lists_in[j * Z + 2 * p], lists_in[j * Z + 2 * p + 1])
            for kb in range(rows // 256):
                hit = jnp.where(row_line == want - kb * 256, 1.0, 0.0).astype(BF)
                oh[j, kb * 256:(kb + 1) * 256, p * LANES:(p + 1) * LANES] = hit
        found = nn(table_ref[...], oh[j])
        for p in range(Z // 2):
            even, odd = pack_pair(found[:, p * LANES:(p + 1) * LANES], low)
            sbuf[j * Z + 2 * p] = even
            sbuf[j * Z + 2 * p + 1] = odd

        def send_rows(q, carry):
            send(sbuf.at[q], rbuf.at[q], send_sem.at[2], row_sem.at[j], shard=peer(q, False))
            return carry

        lax.fori_loop(j * Z + (1 if first else 0), j * Z + Z, send_rows, 0)

    serve(0, True)
    rbuf[0] = sbuf[0]

    def serve_step(j, carry):
        serve(j, False)
        return carry

    lax.fori_loop(1, groups, serve_step, 0)

    slot_line = lax.broadcasted_iota(jnp.int32, (HALF, LANES), 0)

    def count_step(j, carry):
        for i in range(Z):
            base = peer(j * Z + i, True) * HALF
            for c in range(bag_lanes // LANES):
                lanes = slice(c * LANES, (c + 1) * LANES)
                count = jnp.zeros((HALF, LANES), F32)
                for b in range(bags):
                    count = count + jnp.where(slot_line == bag_ref[b:b + 1, lanes] - base, 1.0, 0.0)
                mt[j, i * HALF:(i + 1) * HALF, lanes] = count.astype(BF)
        return carry

    lax.fori_loop(0, groups, count_step, 0)

    wait_all(feat_in.at[pl.ds(1, G - 1)], grp_sem.at[0])
    feat_line = lax.broadcasted_iota(jnp.int32, (features, LANES), 0)
    for k in range(G):
        held = feat_line == feat_in[k]
        pm[:features, k * LANES:(k + 1) * LANES] = jnp.where(held & low1, 1.0, 0.0).astype(BF)
        pm[features:, k * LANES:(k + 1) * LANES] = jnp.where(held & ~low1, 1.0, 0.0).astype(BF)

    pooled[...] = jnp.zeros_like(pooled)

    def pool(j, first):
        if first:
            wait_all(rbuf.at[pl.ds(1, Z - 1)], row_sem.at[j])
        else:
            wait_all(rbuf.at[pl.ds(j * Z, Z)], row_sem.at[j])
        for p in range(Z // 2):
            wide[:, p * LANES:(p + 1) * LANES] = unpack_pair(
                rbuf[j * Z + 2 * p], rbuf[j * Z + 2 * p + 1], low
            )
        pooled[...] += nn(wide[...], mt[j])

    pool(0, True)

    def pool_step(j, carry):
        pool(j, False)
        return carry

    lax.fori_loop(1, groups, pool_step, 0)

    for g in range(G):
        k = group_back(g)
        esend[k] = pooled[:, g * LANES:(g + 1) * LANES].astype(BF)

    def send_pooled(k, carry):
        send(esend.at[k], erecv.at[k], send_sem.at[3], grp_sem.at[1], grp=group_back(k))
        return carry

    lax.fori_loop(1, G, send_pooled, 0)
    erecv[0] = esend[0]
    wait_all(erecv.at[pl.ds(1, G - 1)], grp_sem.at[1])

    arrived = jnp.concatenate([erecv[k] for k in range(G)], axis=1)
    both = nt(arrived, pm[...]).astype(BF)
    lcb = lcb_ref[...]
    projt = projt_ref[...]
    fm = fm_ref[...]
    fmt = fmt_ref[...]
    gain = gain_ref[...]
    lcb_grad = jnp.zeros((features, features), F32)
    proj_grad = jnp.zeros(projt.shape, F32)
    fm_grad = jnp.zeros(fm.shape, F32)
    grads_in = []
    for n in range(2):
        xt = both[:, n * features:(n + 1) * features]
        x = nt(pm[n * features:(n + 1) * features, :], arrived).astype(BF)
        low_rank = nt(xt, projt).astype(BF)
        low_rank_t = nt(projt, xt).astype(BF)
        crossed_t = nn(low_rank_t, xt).astype(BF)
        summed = xt.astype(F32) + nn(xt, lcb) + nn(fmt, crossed_t)
        center = summed - jnp.mean(summed, axis=0, keepdims=True)
        inv_std = lax.rsqrt(jnp.mean(center * center, axis=0, keepdims=True) + norm_epsilon)
        normed = center * inv_std
        inter_ref[n] = (normed * gain).astype(BF)
        scaled = cot_ref[n].astype(F32) * gain
        grad_sum = inv_std * (
            scaled
            - jnp.mean(scaled, axis=0, keepdims=True)
            - normed * jnp.mean(scaled * normed, axis=0, keepdims=True)
        )
        grad_low = grad_sum.astype(BF)
        grad_cross_t = nn(fm, grad_low).astype(BF)
        grad_proj = nt(xt, grad_cross_t).astype(BF)
        grad_proj_t = nt(grad_cross_t, xt).astype(BF)
        fm_grad = fm_grad + nt(crossed_t, grad_low)
        proj_grad = proj_grad + nn(grad_proj_t, xt)
        lcb_grad = lcb_grad + nn(x, grad_low)
        grads_in.append((
            grad_sum + nt(grad_low, lcb) + nn(low_rank, grad_cross_t) + nn(grad_proj, projt)
        ).astype(BF))

    back = nn(jnp.concatenate(grads_in, axis=1), pm[...]).astype(BF)
    for k in range(G):
        gsend[k] = back[:, k * LANES:(k + 1) * LANES]

    def send_back(k, carry):
        send(gsend.at[k], grecv.at[k], send_sem.at[4], grp_sem.at[2], grp=group_ahead(k))
        return carry

    lax.fori_loop(1, G, send_back, 0)
    grecv[0] = gsend[0]

    chunk = w.shape[1] // Z
    flat = w.shape[0] * w.shape[1]
    total[...] = jnp.zeros_like(total)
    total[:features] = lcb_grad
    total[features:features + HALF] = proj_grad
    total[features + HALF:features + 2 * HALF, :width] = fm_grad
    for g in range(G):
        w[g] = total[g * Z * chunk:(g + 1) * Z * chunk]

    def send_w(k, carry):
        to = group_back(k)
        send(w.at[to], k1.at[k], send_sem.at[5], grp_sem.at[3], grp=to)
        return carry

    lax.fori_loop(1, G, send_w, 0)

    wait_all(grecv.at[pl.ds(1, G - 1)], grp_sem.at[2])
    for g in range(G):
        gt[:, g * LANES:(g + 1) * LANES] = grecv[group_back(g)]

    def give(j, first):
        slot_grad = nt(gt[...], mt[j])
        for p in range(Z // 2):
            even, odd = pack_pair(slot_grad[:, p * LANES:(p + 1) * LANES], low)
            hsend[j * Z + 2 * p] = even
            hsend[j * Z + 2 * p + 1] = odd

        def send_grads(q, carry):
            send(hsend.at[q], hrecv.at[q], send_sem.at[6], grad_sem.at[j], shard=peer(q, True))
            return carry

        lax.fori_loop(j * Z + (1 if first else 0), j * Z + Z, send_grads, 0)

    give(0, True)
    hrecv[0] = hsend[0]

    def give_step(j, carry):
        give(j, False)
        return carry

    lax.fori_loop(1, groups, give_step, 0)

    def shard_of(x, z, c):
        return (x * Z + z) * 2 + c

    wait_all(k1.at[pl.ds(1, G - 1)], grp_sem.at[3])
    part = w[me_g]
    for k in range(1, G):
        part = part + k1[k]
    for z in range(Z):
        a2[z] = part[z * chunk:(z + 1) * chunk]

    def send_z(k, carry):
        z = lax.rem(me_z + Z - k, Z)
        send(a2.at[z], k2.at[k], send_sem.at[7], grp_sem.at[4], shard=shard_of(me_x, z, core))
        return carry

    lax.fori_loop(1, Z, send_z, 0)
    wait_all(k2.at[pl.ds(1, Z - 1)], grp_sem.at[4])
    part = a2[me_z]
    for k in range(1, Z):
        part = part + k2[k]
    b3[...] = part
    k3[0] = part
    me_xc = me_x * 2 + core
    XC = X * 2

    def send_xc(k, carry):
        xc = lax.rem(me_xc + XC - k, XC)
        send(b3, k3.at[k], send_sem.at[8], grp_sem.at[5],
             shard=shard_of(lax.div(xc, 2), me_z, lax.rem(xc, 2)))
        return carry

    lax.fori_loop(1, XC, send_xc, 0)
    wait_all(k3.at[pl.ds(1, XC - 1)], grp_sem.at[5])
    part = k3[lax.rem(XC - me_xc, XC)]
    for s in range(1, XC):
        part = part + k3[lax.rem(s + XC - me_xc, XC)]
    c4[...] = part
    k4[0] = part

    def send_z_back(k, carry):
        z = lax.rem(me_z + Z - k, Z)
        send(c4, k4.at[k], send_sem.at[9], grp_sem.at[6], shard=shard_of(me_x, z, core))
        return carry

    lax.fori_loop(1, Z, send_z_back, 0)
    wait_all(k4.at[pl.ds(1, Z - 1)], grp_sem.at[6])
    for z in range(Z):
        d5[z * chunk:(z + 1) * chunk] = k4[lax.rem(z + Z - me_z, Z)]
    k5[0] = d5[...]

    def send_g_back(k, carry):
        send(d5, k5.at[k], send_sem.at[10], grp_sem.at[7], grp=group_back(k))
        return carry

    lax.fori_loop(1, G, send_g_back, 0)

    tacc[...] = jnp.zeros_like(tacc)

    def take(j, first):
        if first:
            wait_all(hrecv.at[pl.ds(1, Z - 1)], grad_sem.at[j])
        else:
            wait_all(hrecv.at[pl.ds(j * Z, Z)], grad_sem.at[j])
        for p in range(Z // 2):
            wide[:, p * LANES:(p + 1) * LANES] = unpack_pair(
                hrecv[j * Z + 2 * p], hrecv[j * Z + 2 * p + 1], low
            )
        per = rows // G
        for g in range(G):
            tacc[g] += nt(wide[...], oh[j, g * per:(g + 1) * per, :])

    take(0, True)

    def take_step(j, carry):
        take(j, False)
        return carry

    lax.fori_loop(1, groups, take_step, 0)

    def send_table(k, carry):
        to = group_back(k)
        jsend[k] = tacc[to].astype(BF)
        send(jsend.at[k], jrecv.at[k], send_sem.at[11], grp_sem.at[8], grp=to)
        return carry

    lax.fori_loop(1, G, send_table, 0)

    wait_all(k5.at[pl.ds(1, G - 1)], grp_sem.at[7])
    span = Z * chunk
    for g in range(G):
        total[g * span:(g + 1) * span] = k5[lax.rem(g + G - me_g, G)]
    lcbg_ref[...] = total[:features]
    projg_ref[...] = total[features:features + HALF]
    fmg_ref[...] = total[features + HALF:features + 2 * HALF, :width]

    wait_all(jrecv.at[pl.ds(1, G - 1)], grp_sem.at[8])
    out = tacc[me_g]
    for k in range(1, G):
        out = out + jrecv[k].astype(F32)
    tgrad_ref[...] = out

    wait_all(lists_in.at[pl.ds(1, S - 1)], send_sem.at[0])
    wait_all(feat_in.at[pl.ds(1, G - 1)], send_sem.at[1])
    wait_all(sbuf.at[pl.ds(1, S - 1)], send_sem.at[2])
    wait_all(esend.at[pl.ds(1, G - 1)], send_sem.at[3])
    wait_all(gsend.at[pl.ds(1, G - 1)], send_sem.at[4])
    wait_all(k1.at[pl.ds(1, G - 1)], send_sem.at[5])
    wait_all(hsend.at[pl.ds(1, S - 1)], send_sem.at[6])
    wait_all(k2.at[pl.ds(1, Z - 1)], send_sem.at[7])
    wait_all(k3.at[pl.ds(1, XC - 1)], send_sem.at[8])
    wait_all(k4.at[pl.ds(1, Z - 1)], send_sem.at[9])
    wait_all(k5.at[pl.ds(1, G - 1)], send_sem.at[10])
    wait_all(jsend.at[pl.ds(1, G - 1)], send_sem.at[11])


def shards(X, Z, emb_table, touched, bag_slots, feat_of_slot, lcb_weight, proj_weight, fm_weight,
           ln_gain, cotangent):
    G = lax.axis_size("grp")
    S = X * Z * 2
    wanted = touched[0, 0]
    lists = jnp.concatenate([wanted, wanted], axis=1).reshape(S, 1, LANES)
    samples, slots, bags = bag_slots.shape
    bag = jnp.pad(jnp.transpose(bag_slots, (2, 0, 1)), ((0, 0), (0, 0), (0, HALF - slots)),
                  constant_values=-1).reshape(bags, samples * HALF)
    feat = jnp.pad(feat_of_slot, ((0, 0), (0, HALF - slots)), constant_values=-1)
    feat = jnp.concatenate([feat, feat], axis=1)
    table_t = emb_table.T
    width, rows = table_t.shape
    features = lcb_weight.shape[0]
    rank = proj_weight.shape[1]
    groups = X * 2
    chunk = -(-(features + 2 * HALF) // (G * Z * 8)) * 8
    vm = pltpu.VMEM
    dma = pltpu.SemaphoreType.DMA
    fold = (width // 2, LANES)
    scratch = [
        vm((S, 1, LANES), jnp.int32),
        vm((G, 1, LANES), jnp.int32),
        vm((groups, rows, Z * HALF), BF),
        vm((groups, Z * HALF, samples * HALF), BF),
        vm((S,) + fold, BF),
        vm((S,) + fold, BF),
        vm((width, Z * HALF), BF),
        vm((width, samples * HALF), F32),
        vm((G, width, LANES), BF),
        vm((G, width, LANES), BF),
        vm((2 * features, G * LANES), BF),
        vm((G, width, LANES), BF),
        vm((G, width, LANES), BF),
        vm((width, samples * HALF), BF),
        vm((S,) + fold, BF),
        vm((S,) + fold, BF),
        vm((G, width, rows // G), F32),
        vm((G, width, rows // G), BF),
        vm((G, width, rows // G), BF),
        vm((G, Z * chunk, features), F32),
        vm((G, Z * chunk, features), F32),
        vm((Z, chunk, features), F32),
        vm((Z, chunk, features), F32),
        vm((chunk, features), F32),
        vm((X * 2, chunk, features), F32),
        vm((chunk, features), F32),
        vm((Z, chunk, features), F32),
        vm((Z * chunk, features), F32),
        vm((G, Z * chunk, features), F32),
        vm((G * Z * chunk, features), F32),
        dma((12,)),
        dma((groups,)),
        dma((groups,)),
        dma((groups,)),
        dma((9,)),
    ]
    whole = pl.BlockSpec(memory_space=pltpu.VMEM)
    inter, tgrad, lcbg, projg, fmg = pl.pallas_call(
        functools.partial(kernel, X, Z, G),
        out_shape=(
            jax.ShapeDtypeStruct((2, width, features), BF),
            jax.ShapeDtypeStruct((width, rows // G), F32),
            jax.ShapeDtypeStruct((features, features), F32),
            jax.ShapeDtypeStruct((rank, features), F32),
            jax.ShapeDtypeStruct((rank, width), F32),
        ),
        in_specs=[whole] * 10,
        out_specs=[whole] * 5,
        scratch_shapes=scratch,
        compiler_params=pltpu.CompilerParams(
            collective_id=0, has_side_effects=True, vmem_limit_bytes=58 * 1024 * 1024
        ),
    )(
        lists, bag, feat, table_t, lcb_weight, proj_weight.T, fm_weight, fm_weight.T,
        ln_gain.reshape(-1, 1), jnp.transpose(cotangent, (0, 2, 1)),
    )
    return (jnp.transpose(inter, (0, 2, 1)), tgrad.T, lcbg, projg.T, fmg)


def solution(mesh):
    S = mesh.shape["shard"]
    Z = mesh.shape["grp"]
    X = S // (2 * Z)
    placed = (
        P("shard", None),
        P("shard", "grp", None, None),
        P("shard", "grp", None),
        P("grp", None),
        P(),
        P(),
        P(),
        P(),
        P(("shard", "grp"), None, None),
    )
    return jax.shard_map(
        functools.partial(shards, X, Z),
        mesh=mesh,
        in_specs=placed,
        out_specs=(P(("shard", "grp"), None, None), P(("shard", "grp"), None), P(), P(), P()),
        check_vma=False,
    )
```

time: 577 us -> 179 us (0.31)
  the two profiles are of different devices: /device:TPU:1 before, /device:TPU:11 now
where the time goes in v1:
time: 179 us
  Pallas kernels  168 us (94%)
  local copies, waits for them, and re-layouts  8.62 us (5%)
  other arithmetic  2.11 us (1%)
    pallas_call x1, Pallas kernels, shards(): pl.pallas_call(functools.partial(kernel, X, Z, G), out_shape=(jax.ShapeDt...  168 us
    unnamed x23, local copies, waits for them, and re-layouts  7.15 us

profile of v1, /device:TPU:11, one launch (start us, length us, event | category | flops | bytes accessed | tf_op | source)
XLA Modules:
  0.0 179.0 jit_solution(13640788564724619452)
XLA Ops:
  0.6 0.0 copy-start.7
  0.6 0.6 copy-done.7
  1.3 0.6 pad_add_fusion.1.feat_ref
  1.9 0.0 copy-start.5
  1.9 1.5 pad_add_fusion
  3.4 0.0 copy-done.5
  3.4 0.0 copy-start.2
  3.4 0.7 reshape.20.bag_ref
  4.1 0.1 copy-done.2
  4.2 0.7 copy.17
  4.9 0.0 copy-start.6
  4.9 0.7 copy-done.6
  5.6 0.8 copy.18.gain_ref
  6.4 167.6 %shard_map.128 = (bf16[2,192,256]{2,1,0:T(8,128)(2,1)}, f32[192,256]{1,0:T(8,128)}, f32[256,256]{1,0:T(8,128)}, f32[64,256]{1,0:T(8,128)}, f32[64,192]{1,0:T(8,128)}) custom-call(s32[64,1,128]{2,1,0:T(1,128)} %bitcast.16, s32[4,1024]{1,0:T(4,128)} %reshape.20.bag_ref, s32[1,128]{1,0:T(1,128)} %pad_add_fusion.1.feat_ref, bf16[192,2048]{1,0:T(8,128)(2,1)} %bitcast.11, ...), custom_call_target="tpu_custom_call" | custom-call | tf_op jit(solution)/shard_map/pallas_call | solution.py:475
  173.9 0.0 copy-start.1
  174.0 1.7 copy.25
  175.6 0.0 copy-done.1
  175.6 0.0 copy-start
  175.6 0.7 copy.26
  176.3 0.3 copy-done
  176.6 0.0 copy-start.4
  176.6 0.7 copy.27
  177.3 0.2 copy-done.4
  177.5 0.0 copy-start.3
  177.5 0.6 copy.28
  178.1 0.2 copy-done.3
  178.4 0.6 copy.29
  (3 shorter events, 0.0 us)
Async XLA Ops:
  0.6 0.7 copy-start.7
  1.9 1.5 copy-start.5
  3.4 0.8 copy-start.2
  4.9 0.7 copy-start.6
  173.9 1.7 copy-start.1
  175.6 1.0 copy-start
  176.6 0.9 copy-start.4
  177.5 0.9 copy-start.3

commit v2 on v1

v2 whole, which is shorter than its diff:
```python
import functools

import jax
import jax.numpy as jnp
from jax import lax
from jax.experimental import pallas as pl
from jax.experimental.pallas import tpu as pltpu
from jax.sharding import PartitionSpec as P

MESH = pl.DeviceIdType.MESH
norm_epsilon = 1e-05
LANES = 128
HALF = 64
BF = jnp.bfloat16
F32 = jnp.float32


def nn(a, b):
    return lax.dot_general(a, b, (((1,), (0,)), ((), ())), preferred_element_type=F32)


def nt(a, b):
    return lax.dot_general(a, b, (((1,), (1,)), ((), ())), preferred_element_type=F32)


def wait_all(ref, sem):
    pltpu.make_async_copy(ref, ref, sem).wait()


def pack_pair(x, low):
    m = x.shape[0] // 2
    turned = pltpu.roll(x, HALF, 1)
    even = jnp.where(low[:m], x[:m], turned[m:])
    odd = jnp.where(low[:m], turned[:m], x[m:])
    return even.astype(BF), odd.astype(BF)


def unpack_pair(even, odd, low):
    m = even.shape[0]
    even, odd = even.astype(F32), odd.astype(F32)
    top = jnp.where(low[:m], even, pltpu.roll(odd, HALF, 1))
    bottom = jnp.where(low[:m], pltpu.roll(even, HALF, 1), odd)
    return jnp.concatenate([top, bottom], axis=0).astype(BF)


def pack_dense(x, lane):
    m = x.shape[0] // 4
    last = x[3 * m:]
    tail = jnp.concatenate([pltpu.roll(last, shift, 1) for shift in (96, 64, 32)], axis=0)
    return jnp.where(lane[:3 * m] < 96, x[:3 * m], tail).astype(BF)


def unpack_dense(packed, lane):
    m = packed.shape[0] // 3
    wide = packed.astype(F32)
    first, second, third = (
        pltpu.roll(wide[i * m:(i + 1) * m], 32 * (i + 1), 1) for i in range(3)
    )
    at = lane[:m]
    last = jnp.where(at < 32, first, jnp.where(at < 64, second, third))
    return jnp.concatenate([wide, last], axis=0).astype(BF)


def kernel(
    X, Z, G,
    lists_ref, bag_ref, feat_ref, table_ref, lcb_ref, projt_ref, fm_ref, gain_ref, cot_ref,
    inter_ref, tgrad_ref, lcbg_ref, projg_ref, fmg_ref,
    l1, r1, r1t, r2, bagl, feat_own, feat_in, oh, mt,
    sbuf0, sbuf1, rbuf0, rbuf1, wide0, wide1, pooled0, pooled1, esend0, esend1, erecv0, erecv1,
    pm, gsend, grecv, gt, hsend0, hsend1, hrecv0, hrecv1, tacc0, tacc1, jsend0, jsend1, jrecv0, jrecv1,
    w, k1, a2, k2, b3, k3, c4, k4, d5, k5, total,
    send_sem, list_sem, row_sem, grad_sem, grp_sem,
):
    S = X * Z * 2
    XC = X * 2
    groups = X * 2
    me_s = lax.axis_index("shard")
    me_g = lax.axis_index("grp")
    core = lax.rem(me_s, 2)
    me_z = lax.rem(lax.div(me_s, 2), Z)
    me_x = lax.div(me_s, 2 * Z)
    me_xc = me_x * 2 + core
    rows = table_ref.shape[1]
    width = table_ref.shape[0]
    features = lcb_ref.shape[0]
    samples, bags, slots = bag_ref.shape
    bag_lanes = bagl.shape[1]
    sbuf, rbuf, wide, pooled = (sbuf0, sbuf1), (rbuf0, rbuf1), (wide0, wide1), (pooled0, pooled1)
    esend, erecv = (esend0, esend1), (erecv0, erecv1)
    hsend, hrecv, tacc = (hsend0, hsend1), (hrecv0, hrecv1), (tacc0, tacc1)
    jsend, jrecv = (jsend0, jsend1), (jrecv0, jrecv1)
    cut = wide0.shape[0]
    parts = (slice(0, cut), slice(cut, width))

    def shard_of(x, z, c):
        return (x * Z + z) * 2 + c

    def peer(q, back):
        i = lax.rem(q, Z)
        j = lax.div(q, Z)
        dc = lax.rem(j, 2)
        dx = lax.rem(lax.div(j, 2) + i, X)
        if back:
            x, z = lax.rem(me_x + X - dx, X), lax.rem(me_z + Z - i, Z)
        else:
            x, z = lax.rem(me_x + dx, X), lax.rem(me_z + i, Z)
        return shard_of(x, z, lax.rem(core + dc, 2))

    def z_back(k):
        return shard_of(me_x, lax.rem(me_z + Z - k, Z), core)

    def xc_back(k):
        x = lax.rem(me_x + X - lax.div(k, 2), X)
        return shard_of(x, me_z, lax.rem(core + lax.rem(k, 2), 2))

    def group_back(k):
        return lax.rem(me_g + G - k, G)

    def group_ahead(k):
        return lax.rem(me_g + k, G)

    def send(src, dst, ssem, rsem, **where):
        pltpu.make_async_remote_copy(
            src_ref=src, dst_ref=dst, send_sem=ssem, recv_sem=rsem,
            device_id=where, device_id_type=MESH,
        ).start()

    def each(count, body, first=1):
        def step(k, carry):
            body(k)
            return carry

        lax.fori_loop(first, count, step, 0)

    barrier = pltpu.get_barrier_semaphore()

    def greet(**where):
        pl.semaphore_signal(barrier, inc=1, device_id=where, device_id_type=MESH)

    each(Z, lambda k: greet(shard=z_back(k)))
    each(XC, lambda k: greet(shard=xc_back(k)))
    each(G, lambda k: greet(grp=group_back(k)))

    lists = jnp.concatenate([lists_ref[...], lists_ref[...]], axis=1)
    for z in range(Z):
        for x in range(X):
            at = (x * Z + z) * 2
            l1[z, 2 * x:2 * x + 2, :] = lists[at:at + 2]

    feat_own[...] = jnp.full(feat_own.shape, -1, jnp.int32)
    for side in range(2):
        feat_own[:, 32 * side:32 * side + 32] = feat_ref[:, :32]
        feat_own[:, 64 + 16 * side:80 + 16 * side] = feat_ref[:, 32:48]
    pl.semaphore_wait(barrier, Z - 1 + XC - 1 + G - 1)

    r1[0] = l1[me_z]

    def send_list(k):
        z = lax.rem(me_z + Z - k, Z)
        send(l1.at[z], r1.at[k], send_sem.at[0], list_sem.at[0], shard=z_back(k))

    each(Z, send_list)
    each(G, lambda k: send(feat_own, feat_in.at[k], send_sem.at[1], grp_sem.at[0], grp=group_back(k)))
    feat_in[0] = feat_own[...]
    wait_all(r1.at[pl.ds(1, Z - 1)], list_sem.at[0])
    for xc in range(XC):
        for z in range(Z):
            r1t[xc, z:z + 1, :] = r1[z, xc:xc + 1, :]

    def send_list_on(k):
        xc = lax.rem(me_x + X - lax.div(k, 2), X) * 2 + lax.rem(core + lax.rem(k, 2), 2)
        send(r1t.at[xc], r2.at[k], send_sem.at[2], list_sem.at[1], shard=xc_back(k))

    each(XC, send_list_on)
    r2[0] = r1t[me_xc]
    wait_all(r2.at[pl.ds(1, XC - 1)], list_sem.at[1])

    low1 = lax.broadcasted_iota(jnp.int32, (1, LANES), 1) < HALF
    low = lax.broadcasted_iota(jnp.int32, (cut // 2, LANES), 1) < HALF
    lane = lax.broadcasted_iota(jnp.int32, (width, LANES), 1)
    row_line = lax.broadcasted_iota(jnp.int32, (256, LANES), 0)

    def serve(j, first):
        def want_of(i):
            return r2[lax.rem(lax.div(j, 2) + i, X) * 2 + lax.rem(j, 2), i:i + 1, :]

        for p in range(Z // 2):
            want = jnp.where(low1, want_of(2 * p), want_of(2 * p + 1))
            for kb in range(rows // 256):
                hit = jnp.where(row_line == want - kb * 256, 1.0, 0.0).astype(BF)
                oh[j, kb * 256:(kb + 1) * 256, p * LANES:(p + 1) * LANES] = hit
        found = nn(table_ref[...], oh[j])
        for p in range(Z // 2):
            for h in range(2):
                even, odd = pack_pair(found[parts[h], p * LANES:(p + 1) * LANES], low)
                sbuf[h][j * Z + 2 * p] = even
                sbuf[h][j * Z + 2 * p + 1] = odd

        each(j * Z + Z, lambda q: send(sbuf0.at[q], rbuf0.at[q], send_sem.at[3], row_sem.at[j],
                                       shard=peer(q, False)),
             first=j * Z + (1 if first else 0))

    serve(0, True)
    each(groups, lambda j: serve(j, False))
    each(S, lambda q: send(sbuf1.at[q], rbuf1.at[q], send_sem.at[4], row_sem.at[groups + lax.div(q, Z)],
                           shard=peer(q, False)))
    for h in range(2):
        rbuf[h][0] = sbuf[h][0]

    bagl[...] = jnp.full(bagl.shape, -1, jnp.int32)
    for n in range(samples):
        at = n // 2 * LANES
        side = n % 2
        bagl[:, at + 32 * side:at + 32 * side + 32] = bag_ref[n, :, :32]
        bagl[:, at + 64 + 16 * side:at + 80 + 16 * side] = bag_ref[n, :, 32:48]
    slot_line = lax.broadcasted_iota(jnp.int32, (HALF, LANES), 0)

    def count(j):
        for i in range(Z):
            base = peer(j * Z + i, True) * HALF
            for c in range(bag_lanes // LANES):
                lanes = slice(c * LANES, (c + 1) * LANES)
                times = jnp.zeros((HALF, LANES), F32)
                for b in range(bags):
                    times = times + jnp.where(slot_line == bagl[b:b + 1, lanes] - base, 1.0, 0.0)
                mt[j, i * HALF:(i + 1) * HALF, lanes] = times.astype(BF)

    each(groups, count, first=0)

    wait_all(feat_in.at[pl.ds(1, G - 1)], grp_sem.at[0])
    feat_line = lax.broadcasted_iota(jnp.int32, (features, LANES), 0)
    lane1 = lax.broadcasted_iota(jnp.int32, (1, LANES), 1)
    second = ((lane1 >= 32) & (lane1 < 64)) | ((lane1 >= 80) & (lane1 < 96))
    for k in range(G):
        held = feat_line == feat_in[k]
        pm[:features, k * LANES:(k + 1) * LANES] = jnp.where(held & ~second, 1.0, 0.0).astype(BF)
        pm[features:, k * LANES:(k + 1) * LANES] = jnp.where(held & second, 1.0, 0.0).astype(BF)
    eye = jnp.where(
        lax.broadcasted_iota(jnp.int32, (width, width), 0) == lax.broadcasted_iota(jnp.int32, (width, width), 1),
        1.0, 0.0,
    )
    fm = fm_ref[...]
    fmt = nt(eye.astype(BF), fm).astype(BF)
    gain = jnp.sum(eye * gain_ref[...], axis=1, keepdims=True)

    def pool(h, j, first):
        at = j * Z
        if first:
            wait_all(rbuf[h].at[pl.ds(1, Z - 1)], row_sem.at[h * groups + j])
        else:
            wait_all(rbuf[h].at[pl.ds(at, Z)], row_sem.at[h * groups + j])
        for p in range(Z // 2):
            wide[h][:, p * LANES:(p + 1) * LANES] = unpack_pair(
                rbuf[h][at + 2 * p], rbuf[h][at + 2 * p + 1], low
            )
        now = nn(wide[h][...], mt[j])
        pooled[h][...] = now if first else pooled[h][...] + now

    for h in range(2):
        pool(h, 0, True)
        each(groups, lambda j, h=h: pool(h, j, False))
        for g in range(G):
            esend[h][group_back(g)] = pack_dense(pooled[h][:, g * LANES:(g + 1) * LANES], lane)
        each(G, lambda k, h=h: send(esend[h].at[k], erecv[h].at[k], send_sem.at[5 + h], grp_sem.at[1 + h],
                                    grp=group_back(k)))
        erecv[h][0] = esend[h][0]
    for h in range(2):
        wait_all(erecv[h].at[pl.ds(1, G - 1)], grp_sem.at[1 + h])

    arrived = jnp.concatenate([
        jnp.concatenate([unpack_dense(erecv[h][k], lane) for h in range(2)], axis=0) for k in range(G)
    ], axis=1)
    both = nt(arrived, pm[...]).astype(BF)
    lcb = lcb_ref[...]
    projt = projt_ref[...]
    lcb_grad = jnp.zeros((features, features), F32)
    proj_grad = jnp.zeros(projt.shape, F32)
    fm_grad = jnp.zeros(fm.shape, F32)
    grads_in = []
    for n in range(2):
        xt = both[:, n * features:(n + 1) * features]
        x = nt(pm[n * features:(n + 1) * features, :], arrived).astype(BF)
        low_rank = nt(xt, projt).astype(BF)
        low_rank_t = nt(projt, xt).astype(BF)
        crossed_t = nn(low_rank_t, xt).astype(BF)
        summed = xt.astype(F32) + nn(xt, lcb) + nn(fmt, crossed_t)
        center = summed - jnp.mean(summed, axis=0, keepdims=True)
        inv_std = lax.rsqrt(jnp.mean(center * center, axis=0, keepdims=True) + norm_epsilon)
        normed = center * inv_std
        inter_ref[n] = (normed * gain).astype(BF)
        scaled = cot_ref[n].astype(F32) * gain
        grad_sum = inv_std * (
            scaled
            - jnp.mean(scaled, axis=0, keepdims=True)
            - normed * jnp.mean(scaled * normed, axis=0, keepdims=True)
        )
        grad_low = grad_sum.astype(BF)
        grad_cross_t = nn(fm, grad_low).astype(BF)
        grad_proj = nt(xt, grad_cross_t).astype(BF)
        grad_proj_t = nt(grad_cross_t, xt).astype(BF)
        fm_grad = fm_grad + nt(crossed_t, grad_low)
        proj_grad = proj_grad + nn(grad_proj_t, xt)
        lcb_grad = lcb_grad + nn(x, grad_low)
        grads_in.append((
            grad_sum + nt(grad_low, lcb) + nn(low_rank, grad_cross_t) + nn(grad_proj, projt)
        ).astype(BF))

    back = nn(jnp.concatenate(grads_in, axis=1), pm[...])
    for k in range(G):
        gsend[k] = pack_dense(back[:, k * LANES:(k + 1) * LANES], lane)
    each(G, lambda k: send(gsend.at[k], grecv.at[k], send_sem.at[7], grp_sem.at[3], grp=group_ahead(k)))
    grecv[0] = gsend[0]

    chunk = a2.shape[1]
    span = Z * chunk
    total[...] = jnp.zeros_like(total)
    total[:features] = lcb_grad
    total[features:features + HALF] = proj_grad
    total[features + HALF:features + 2 * HALF, :width] = fm_grad
    for g in range(G):
        w[g] = total[g * span:(g + 1) * span].astype(BF)
    each(G, lambda k: send(w.at[group_back(k)], k1.at[k], send_sem.at[8], grp_sem.at[4], grp=group_back(k)))

    wait_all(grecv.at[pl.ds(1, G - 1)], grp_sem.at[3])
    for g in range(G):
        gt[:, g * LANES:(g + 1) * LANES] = unpack_dense(grecv[group_back(g)], lane)

    def give(j, first):
        slot_grad = nt(gt[...], mt[j])
        for p in range(Z // 2):
            for h in range(2):
                even, odd = pack_pair(slot_grad[parts[h], p * LANES:(p + 1) * LANES], low)
                hsend[h][j * Z + 2 * p] = even
                hsend[h][j * Z + 2 * p + 1] = odd

        each(j * Z + Z, lambda q: send(hsend0.at[q], hrecv0.at[q], send_sem.at[9], grad_sem.at[j],
                                       shard=peer(q, True)),
             first=j * Z + (1 if first else 0))

    def give_some(step, steps):
        first = step * groups // steps
        last = (step + 1) * groups // steps
        if first == 0:
            give(0, True)
            first = 1
        each(last, lambda j: give(j, False), first=first)

    give_some(0, 4)
    wait_all(k1.at[pl.ds(1, G - 1)], grp_sem.at[4])
    part = w[me_g].astype(F32)
    for k in range(1, G):
        part = part + k1[k].astype(F32)
    for z in range(Z):
        a2[z] = part[z * chunk:(z + 1) * chunk]
    each(Z, lambda k: send(a2.at[lax.rem(me_z + Z - k, Z)], k2.at[k], send_sem.at[10], grp_sem.at[5],
                           shard=z_back(k)))

    give_some(1, 4)
    wait_all(k2.at[pl.ds(1, Z - 1)], grp_sem.at[5])
    part = a2[me_z]
    for k in range(1, Z):
        part = part + k2[k]
    b3[...] = part
    k3[0] = part
    each(XC, lambda k: send(b3, k3.at[k], send_sem.at[11], grp_sem.at[6], shard=xc_back(k)))

    give_some(2, 4)
    wait_all(k3.at[pl.ds(1, XC - 1)], grp_sem.at[6])

    def from_xc(s):
        dx = lax.rem(s // 2 + X - me_x, X)
        return k3[dx * 2 + lax.rem(s % 2 + core, 2)]

    part = from_xc(0)
    for s in range(1, XC):
        part = part + from_xc(s)
    c4[...] = part
    k4[0] = part
    each(Z, lambda k: send(c4, k4.at[k], send_sem.at[12], grp_sem.at[7], shard=z_back(k)))

    give_some(3, 4)
    each(S, lambda q: send(hsend1.at[q], hrecv1.at[q], send_sem.at[13], grad_sem.at[groups + lax.div(q, Z)],
                           shard=peer(q, True)))
    for h in range(2):
        hrecv[h][0] = hsend[h][0]

    wait_all(k4.at[pl.ds(1, Z - 1)], grp_sem.at[7])
    for z in range(Z):
        d5[z * chunk:(z + 1) * chunk] = k4[lax.rem(z + Z - me_z, Z)].astype(BF)
    k5[0] = d5[...]
    each(G, lambda k: send(d5, k5.at[k], send_sem.at[14], grp_sem.at[8], grp=group_back(k)))

    per = rows // G

    def take(h, j, first):
        at = j * Z
        if first:
            wait_all(hrecv[h].at[pl.ds(1, Z - 1)], grad_sem.at[h * groups + j])
        else:
            wait_all(hrecv[h].at[pl.ds(at, Z)], grad_sem.at[h * groups + j])
        for p in range(Z // 2):
            wide[h][:, p * LANES:(p + 1) * LANES] = unpack_pair(
                hrecv[h][at + 2 * p], hrecv[h][at + 2 * p + 1], low
            )
        for g in range(G):
            now = nt(wide[h][...], oh[j, g * per:(g + 1) * per, :])
            tacc[h][g] = now if first else tacc[h][g] + now

    def send_table(k, h):
        to = group_back(k)
        jsend[h][k] = tacc[h][to].astype(BF)
        send(jsend[h].at[k], jrecv[h].at[k], send_sem.at[15 + h], grp_sem.at[9 + h], grp=to)

    for h in range(2):
        take(h, 0, True)
        each(groups, lambda j, h=h: take(h, j, False))
        each(G, lambda k, h=h: send_table(k, h))

    wait_all(k5.at[pl.ds(1, G - 1)], grp_sem.at[8])
    for g in range(G):
        total[g * span:(g + 1) * span] = k5[lax.rem(g + G - me_g, G)].astype(F32)
    lcbg_ref[...] = total[:features]
    projg_ref[...] = total[features:features + HALF]
    fmg_ref[...] = total[features + HALF:features + 2 * HALF, :width]

    for h in range(2):
        wait_all(jrecv[h].at[pl.ds(1, G - 1)], grp_sem.at[9 + h])
        out = tacc[h][me_g]
        for k in range(1, G):
            out = out + jrecv[h][k].astype(F32)
        tgrad_ref[parts[h], :] = out

    wait_all(r1.at[pl.ds(1, Z - 1)], send_sem.at[0])
    wait_all(feat_in.at[pl.ds(1, G - 1)], send_sem.at[1])
    wait_all(r2.at[pl.ds(1, XC - 1)], send_sem.at[2])
    wait_all(sbuf0.at[pl.ds(1, S - 1)], send_sem.at[3])
    wait_all(sbuf1.at[pl.ds(1, S - 1)], send_sem.at[4])
    wait_all(esend0.at[pl.ds(1, G - 1)], send_sem.at[5])
    wait_all(esend1.at[pl.ds(1, G - 1)], send_sem.at[6])
    wait_all(gsend.at[pl.ds(1, G - 1)], send_sem.at[7])
    wait_all(k1.at[pl.ds(1, G - 1)], send_sem.at[8])
    wait_all(hsend0.at[pl.ds(1, S - 1)], send_sem.at[9])
    wait_all(k2.at[pl.ds(1, Z - 1)], send_sem.at[10])
    wait_all(k3.at[pl.ds(1, XC - 1)], send_sem.at[11])
    wait_all(k4.at[pl.ds(1, Z - 1)], send_sem.at[12])
    wait_all(hsend1.at[pl.ds(1, S - 1)], send_sem.at[13])
    wait_all(k5.at[pl.ds(1, G - 1)], send_sem.at[14])
    wait_all(jsend0.at[pl.ds(1, G - 1)], send_sem.at[15])
    wait_all(jsend1.at[pl.ds(1, G - 1)], send_sem.at[16])


def hand_over(*refs):
    half = len(refs) // 2
    for i in range(half):
        refs[half + i][...] = refs[i][...]


def shards(X, Z, emb_table, touched, bag_slots, feat_of_slot, lcb_weight, proj_weight, fm_weight,
           ln_gain, cotangent):
    G = lax.axis_size("grp")
    S = X * Z * 2
    XC = X * 2
    samples, slots, bags = bag_slots.shape
    table_t = emb_table.T
    width, rows = table_t.shape
    features = lcb_weight.shape[0]
    rank = proj_weight.shape[1]
    groups = X * 2
    bag_lanes = samples // 2 * LANES
    chunk = -(-(features + 2 * HALF) // (G * Z * 8)) * 8
    cut = width * 2 // 3
    heights = (cut, width - cut)
    vm = pltpu.VMEM
    dma = pltpu.SemaphoreType.DMA
    per = rows // G

    def two(shape_of, kind):
        return [vm(shape_of(height), kind) for height in heights]

    scratch = [
        vm((Z, XC, LANES), jnp.int32),
        vm((Z, XC, LANES), jnp.int32),
        vm((XC, Z, LANES), jnp.int32),
        vm((XC, Z, LANES), jnp.int32),
        vm((bags, bag_lanes), jnp.int32),
        vm((1, LANES), jnp.int32),
        vm((G, 1, LANES), jnp.int32),
        vm((groups, rows, Z * HALF), BF),
        vm((groups, Z * HALF, bag_lanes), BF),
        *two(lambda m: (S, m // 2, LANES), BF),
        *two(lambda m: (S, m // 2, LANES), BF),
        *two(lambda m: (m, Z * HALF), BF),
        *two(lambda m: (m, bag_lanes), F32),
        *two(lambda m: (G, m * 3 // 4, LANES), BF),
        *two(lambda m: (G, m * 3 // 4, LANES), BF),
        vm((2 * features, G * LANES), BF),
        vm((G, width * 3 // 4, LANES), BF),
        vm((G, width * 3 // 4, LANES), BF),
        vm((width, bag_lanes), BF),
        *two(lambda m: (S, m // 2, LANES), BF),
        *two(lambda m: (S, m // 2, LANES), BF),
        *two(lambda m: (G, m, per), F32),
        *two(lambda m: (G, m, per), BF),
        *two(lambda m: (G, m, per), BF),
        vm((G, Z * chunk, features), BF),
        vm((G, Z * chunk, features), BF),
        vm((Z, chunk, features), F32),
        vm((Z, chunk, features), F32),
        vm((chunk, features), F32),
        vm((XC, chunk, features), F32),
        vm((chunk, features), F32),
        vm((Z, chunk, features), F32),
        vm((Z * chunk, features), BF),
        vm((G, Z * chunk, features), BF),
        vm((G * Z * chunk, features), F32),
        dma((17,)),
        dma((2,)),
        dma((2 * groups,)),
        dma((2 * groups,)),
        dma((11,)),
    ]
    whole = pl.BlockSpec(memory_space=pltpu.VMEM)
    shapes = (
        jax.ShapeDtypeStruct((2, width, features), BF),
        jax.ShapeDtypeStruct((width, per), F32),
        jax.ShapeDtypeStruct((features, features), F32),
        jax.ShapeDtypeStruct((rank, features), F32),
        jax.ShapeDtypeStruct((rank, width), F32),
    )
    results = pl.pallas_call(
        functools.partial(kernel, X, Z, G),
        out_shape=shapes,
        in_specs=[whole] * 9,
        out_specs=[whole] * 5,
        scratch_shapes=scratch,
        compiler_params=pltpu.CompilerParams(
            collective_id=0, has_side_effects=True, vmem_limit_bytes=58 * 1024 * 1024
        ),
    )(
        touched.reshape(S, HALF), jnp.transpose(bag_slots, (0, 2, 1)), feat_of_slot, table_t, lcb_weight,
        proj_weight.T, fm_weight, ln_gain.reshape(1, -1), jnp.transpose(cotangent, (0, 2, 1)),
    )
    inter, tgrad, lcbg, projg, fmg = pl.pallas_call(
        hand_over,
        out_shape=shapes,
        in_specs=[whole] * 5,
        out_specs=[whole] * 5,
    )(*results)
    return (jnp.transpose(inter, (0, 2, 1)), tgrad.T, lcbg, projg.T, fmg)


def solution(mesh):
    S = mesh.shape["shard"]
    Z = mesh.shape["grp"]
    X = S // (2 * Z)
    placed = (
        P("shard", None),
        P("shard", "grp", None, None),
        P("shard", "grp", None),
        P("grp", None),
        P(),
        P(),
        P(),
        P(),
        P(("shard", "grp"), None, None),
    )
    return jax.shard_map(
        functools.partial(shards, X, Z),
        mesh=mesh,
        in_specs=placed,
        out_specs=(P(("shard", "grp"), None, None), P(("shard", "grp"), None), P(), P(), P()),
        check_vma=False,
    )
```

time: 179 us -> 136 us (0.76)
  the two profiles are of different devices: /device:TPU:11 before, /device:TPU:1 now
where the time goes in v2:
time: 136 us
  Pallas kernels  136 us (100%)
    pallas_call x1, Pallas kernels, shards(): pl.pallas_call(functools.partial(kernel, X, Z, G), out_shape=shapes, in_s...  134 us

profile of v2, /device:TPU:1, one launch (start us, length us, event | category | flops | bytes accessed | tf_op | source)
XLA Modules:
  0.0 136.2 jit_solution(7208768935316208330)
XLA Ops:
  0.6 133.5 %shard_map.128 = (bf16[2,192,256]{2,1,0:T(8,128)(2,1)}, f32[192,256]{1,0:T(8,128)}, f32[256,256]{1,0:T(8,128)}, f32[64,256]{1,0:T(8,128)}, f32[64,192]{1,0:T(8,128)}) custom-call(s32[64,64]{1,0:T(8,128)} %bitcast.11, s32[16,4,48]{2,1,0:T(4,128)} %bitcast.12, s32[1,48]{1,0:T(1,128)} %feat_ref.1, bf16[192,2048]{1,0:T(8,128)(2,1)} %bitcast.9, ...), custom_call_target="tpu_custom_call" | custom-call | tf_op jit(solution)/shard_map/pallas_call | solution.py:530
  134.1 2.1 %shard_map.129 = (bf16[2,192,256]{2,1,0:T(8,128)(2,1)}, f32[192,256]{1,0:T(8,128)}, f32[256,256]{1,0:T(8,128)}, f32[64,256]{1,0:T(8,128)}, f32[64,192]{1,0:T(8,128)}) custom-call(bf16[2,192,256]{2,1,0:T(8,128)(2,1)} %get-tuple-element.15.refs_0_, f32[192,256]{1,0:T(8,128)} %get-tuple-element.16.refs_1_, f32[256,256]{1,0:T(8,128)} %get-tuple-element.17.refs_2_, ...), custom_call_target="tpu_custom_call" | custom-call | tf_op jit(solution)/shard_map/pallas_call | solution.py:543

commit v3 on v2

--- a/solution.py
+++ b/solution.py
@@ -67,7 +67,8 @@
     inter_ref, tgrad_ref, lcbg_ref, projg_ref, fmg_ref,
     l1, r1, r1t, r2, bagl, feat_own, feat_in, oh, mt,
     sbuf0, sbuf1, rbuf0, rbuf1, wide0, wide1, pooled0, pooled1, esend0, esend1, erecv0, erecv1,
-    pm, gsend, grecv, gt, hsend0, hsend1, hrecv0, hrecv1, tacc0, tacc1, jsend0, jsend1, jrecv0, jrecv1,
+    pm, gsend0, gsend1, grecv0, grecv1, gt, hsend0, hsend1, hsend2, hrecv0, hrecv1, hrecv2,
+    tacc0, tacc1, tacc2, jsend0, jsend1, jsend2, jrecv0, jrecv1, jrecv2,
     w, k1, a2, k2, b3, k3, c4, k4, d5, k5, total,
     send_sem, list_sem, row_sem, grad_sem, grp_sem,
 ):
@@ -87,8 +88,13 @@
     bag_lanes = bagl.shape[1]
     sbuf, rbuf, wide, pooled = (sbuf0, sbuf1), (rbuf0, rbuf1), (wide0, wide1), (pooled0, pooled1)
     esend, erecv = (esend0, esend1), (erecv0, erecv1)
-    hsend, hrecv, tacc = (hsend0, hsend1), (hrecv0, hrecv1), (tacc0, tacc1)
-    jsend, jrecv = (jsend0, jsend1), (jrecv0, jrecv1)
+    gsend, grecv = (gsend0, gsend1), (grecv0, grecv1)
+    hsend, hrecv, tacc = (hsend0, hsend1, hsend2), (hrecv0, hrecv1, hrecv2), (tacc0, tacc1, tacc2)
+    jsend, jrecv = (jsend0, jsend1, jsend2), (jrecv0, jrecv1, jrecv2)
+    lead = tacc0.shape[1]
+    mid = lead + tacc1.shape[1]
+    back_parts = (slice(0, lead), slice(lead, width))
+    grad_parts = (slice(0, lead), slice(lead, mid), slice(mid, width))
     cut = wide0.shape[0]
     parts = (slice(0, cut), slice(cut, width))
 
@@ -99,7 +105,7 @@
         i = lax.rem(q, Z)
         j = lax.div(q, Z)
         dc = lax.rem(j, 2)
-        dx = lax.rem(lax.div(j, 2) + i, X)
+        dx = lax.div(j, 2)
         if back:
             x, z = lax.rem(me_x + X - dx, X), lax.rem(me_z + Z - i, Z)
         else:
@@ -169,11 +175,10 @@
 
     def send_list_on(k):
         xc = lax.rem(me_x + X - lax.div(k, 2), X) * 2 + lax.rem(core + lax.rem(k, 2), 2)
-        send(r1t.at[xc], r2.at[k], send_sem.at[2], list_sem.at[1], shard=xc_back(k))
+        send(r1t.at[xc], r2.at[k], send_sem.at[2], list_sem.at[k], shard=xc_back(k))
 
     each(XC, send_list_on)
     r2[0] = r1t[me_xc]
-    wait_all(r2.at[pl.ds(1, XC - 1)], list_sem.at[1])
 
     low1 = lax.broadcasted_iota(jnp.int32, (1, LANES), 1) < HALF
     low = lax.broadcasted_iota(jnp.int32, (cut // 2, LANES), 1) < HALF
@@ -181,11 +186,10 @@
     row_line = lax.broadcasted_iota(jnp.int32, (256, LANES), 0)
 
     def serve(j, first):
-        def want_of(i):
-            return r2[lax.rem(lax.div(j, 2) + i, X) * 2 + lax.rem(j, 2), i:i + 1, :]
-
+        if not first:
+            wait_all(r2.at[j], list_sem.at[j])
         for p in range(Z // 2):
-            want = jnp.where(low1, want_of(2 * p), want_of(2 * p + 1))
+            want = jnp.where(low1, r2[j, 2 * p:2 * p + 1, :], r2[j, 2 * p + 1:2 * p + 2, :])
             for kb in range(rows // 256):
                 hit = jnp.where(row_line == want - kb * 256, 1.0, 0.0).astype(BF)
                 oh[j, kb * 256:(kb + 1) * 256, p * LANES:(p + 1) * LANES] = hit
@@ -273,13 +277,10 @@
     both = nt(arrived, pm[...]).astype(BF)
     lcb = lcb_ref[...]
     projt = projt_ref[...]
-    lcb_grad = jnp.zeros((features, features), F32)
-    proj_grad = jnp.zeros(projt.shape, F32)
-    fm_grad = jnp.zeros(fm.shape, F32)
     grads_in = []
+    later = []
     for n in range(2):
         xt = both[:, n * features:(n + 1) * features]
-        x = nt(pm[n * features:(n + 1) * features, :], arrived).astype(BF)
         low_rank = nt(xt, projt).astype(BF)
         low_rank_t = nt(projt, xt).astype(BF)
         crossed_t = nn(low_rank_t, xt).astype(BF)
@@ -297,98 +298,68 @@
         grad_low = grad_sum.astype(BF)
         grad_cross_t = nn(fm, grad_low).astype(BF)
         grad_proj = nt(xt, grad_cross_t).astype(BF)
+        grads_in.append((
+            grad_sum + nt(grad_low, lcb) + nn(low_rank, grad_cross_t) + nn(grad_proj, projt)
+        ).astype(BF))
+        later.append((xt, crossed_t, grad_low, grad_cross_t))
+
+    grad_in = jnp.concatenate(grads_in, axis=1)
+
+    def send_back(h):
+        back = nn(grad_in[back_parts[h]], pm[...])
+        for k in range(G):
+            gsend[h][k] = pack_dense(back[:, k * LANES:(k + 1) * LANES], lane)
+        each(G, lambda k: send(gsend[h].at[k], grecv[h].at[k], send_sem.at[7 + h], grp_sem.at[3 + h],
+                               grp=group_ahead(k)))
+        grecv[h][0] = gsend[h][0]
+
+    send_back(0)
+
+    lcb_grad = jnp.zeros((features, features), F32)
+    proj_grad = jnp.zeros(projt.shape, F32)
+    fm_grad = jnp.zeros(fm.shape, F32)
+    for n in range(2):
+        xt, crossed_t, grad_low, grad_cross_t = later[n]
+        x = nt(pm[n * features:(n + 1) * features, :], arrived).astype(BF)
         grad_proj_t = nt(grad_cross_t, xt).astype(BF)
         fm_grad = fm_grad + nt(crossed_t, grad_low)
         proj_grad = proj_grad + nn(grad_proj_t, xt)
         lcb_grad = lcb_grad + nn(x, grad_low)
-        grads_in.append((
-            grad_sum + nt(grad_low, lcb) + nn(low_rank, grad_cross_t) + nn(grad_proj, projt)
-        ).astype(BF))
-
-    back = nn(jnp.concatenate(grads_in, axis=1), pm[...])
-    for k in range(G):
-        gsend[k] = pack_dense(back[:, k * LANES:(k + 1) * LANES], lane)
-    each(G, lambda k: send(gsend.at[k], grecv.at[k], send_sem.at[7], grp_sem.at[3], grp=group_ahead(k)))
-    grecv[0] = gsend[0]
-
     chunk = a2.shape[1]
-    span = Z * chunk
+    span = w.shape[1]
     total[...] = jnp.zeros_like(total)
     total[:features] = lcb_grad
     total[features:features + HALF] = proj_grad
     total[features + HALF:features + 2 * HALF, :width] = fm_grad
     for g in range(G):
         w[g] = total[g * span:(g + 1) * span].astype(BF)
-    each(G, lambda k: send(w.at[group_back(k)], k1.at[k], send_sem.at[8], grp_sem.at[4], grp=group_back(k)))
-
-    wait_all(grecv.at[pl.ds(1, G - 1)], grp_sem.at[3])
-    for g in range(G):
-        gt[:, g * LANES:(g + 1) * LANES] = unpack_dense(grecv[group_back(g)], lane)
-
-    def give(j, first):
-        slot_grad = nt(gt[...], mt[j])
+    each(G, lambda k: send(w.at[group_back(k)], k1.at[k], send_sem.at[9], grp_sem.at[5], grp=group_back(k)))
+    send_back(1)
+
+    def bring(h):
+        wait_all(grecv[h].at[pl.ds(1, G - 1)], grp_sem.at[3 + h])
+        for g in range(G):
+            gt[back_parts[h], g * LANES:(g + 1) * LANES] = unpack_dense(grecv[h][group_back(g)], lane)
+
+    bring(0)
+
+    def give(h, j, first):
+        slot_grad = nt(gt[grad_parts[h], :], mt[j])
         for p in range(Z // 2):
-            for h in range(2):
-                even, odd = pack_pair(slot_grad[parts[h], p * LANES:(p + 1) * LANES], low)
-                hsend[h][j * Z + 2 * p] = even
-                hsend[h][j * Z + 2 * p + 1] = odd
-
-        each(j * Z + Z, lambda q: send(hsend0.at[q], hrecv0.at[q], send_sem.at[9], grad_sem.at[j],
-                                       shard=peer(q, True)),
+            even, odd = pack_pair(slot_grad[:, p * LANES:(p + 1) * LANES], low)
+            hsend[h][j * Z + 2 * p] = even
+            hsend[h][j * Z + 2 * p + 1] = odd
+        if first:
+            hrecv[h][0] = hsend[h][0]
+        each(j * Z + Z, lambda q: send(hsend[h].at[q], hrecv[h].at[q], send_sem.at[10 + h],
+                                       grad_sem.at[h * groups + j], shard=peer(q, True)),
              first=j * Z + (1 if first else 0))
 
-    def give_some(step, steps):
-        first = step * groups // steps
-        last = (step + 1) * groups // steps
+    def give_some(h, first, last):
         if first == 0:
-            give(0, True)
+            give(h, 0, True)
             first = 1
-        each(last, lambda j: give(j, False), first=first)
-
-    give_some(0, 4)
-    wait_all(k1.at[pl.ds(1, G - 1)], grp_sem.at[4])
-    part = w[me_g].astype(F32)
-    for k in range(1, G):
-        part = part + k1[k].astype(F32)
-    for z in range(Z):
-        a2[z] = part[z * chunk:(z + 1) * chunk]
-    each(Z, lambda k: send(a2.at[lax.rem(me_z + Z - k, Z)], k2.at[k], send_sem.at[10], grp_sem.at[5],
-                           shard=z_back(k)))
-
-    give_some(1, 4)
-    wait_all(k2.at[pl.ds(1, Z - 1)], grp_sem.at[5])
-    part = a2[me_z]
-    for k in range(1, Z):
-        part = part + k2[k]
-    b3[...] = part
-    k3[0] = part
-    each(XC, lambda k: send(b3, k3.at[k], send_sem.at[11], grp_sem.at[6], shard=xc_back(k)))
-
-    give_some(2, 4)
-    wait_all(k3.at[pl.ds(1, XC - 1)], grp_sem.at[6])
-
-    def from_xc(s):
-        dx = lax.rem(s // 2 + X - me_x, X)
-        return k3[dx * 2 + lax.rem(s % 2 + core, 2)]
-
-    part = from_xc(0)
-    for s in range(1, XC):
-        part = part + from_xc(s)
-    c4[...] = part
-    k4[0] = part
-    each(Z, lambda k: send(c4, k4.at[k], send_sem.at[12], grp_sem.at[7], shard=z_back(k)))
-
-    give_some(3, 4)
-    each(S, lambda q: send(hsend1.at[q], hrecv1.at[q], send_sem.at[13], grad_sem.at[groups + lax.div(q, Z)],
-                           shard=peer(q, True)))
-    for h in range(2):
-        hrecv[h][0] = hsend[h][0]
-
-    wait_all(k4.at[pl.ds(1, Z - 1)], grp_sem.at[7])
-    for z in range(Z):
-        d5[z * chunk:(z + 1) * chunk] = k4[lax.rem(z + Z - me_z, Z)].astype(BF)
-    k5[0] = d5[...]
-    each(G, lambda k: send(d5, k5.at[k], send_sem.at[14], grp_sem.at[8], grp=group_back(k)))
+        each(last, lambda j: give(h, j, False), first=first)
 
     per = rows // G
 
@@ -398,37 +369,88 @@
             wait_all(hrecv[h].at[pl.ds(1, Z - 1)], grad_sem.at[h * groups + j])
         else:
             wait_all(hrecv[h].at[pl.ds(at, Z)], grad_sem.at[h * groups + j])
+        m = tacc[h].shape[1]
         for p in range(Z // 2):
-            wide[h][:, p * LANES:(p + 1) * LANES] = unpack_pair(
+            wide0[:m, p * LANES:(p + 1) * LANES] = unpack_pair(
                 hrecv[h][at + 2 * p], hrecv[h][at + 2 * p + 1], low
             )
         for g in range(G):
-            now = nt(wide[h][...], oh[j, g * per:(g + 1) * per, :])
+            now = nt(wide0[:m, :], oh[j, g * per:(g + 1) * per, :])
             tacc[h][g] = now if first else tacc[h][g] + now
 
-    def send_table(k, h):
-        to = group_back(k)
-        jsend[h][k] = tacc[h][to].astype(BF)
-        send(jsend[h].at[k], jrecv[h].at[k], send_sem.at[15 + h], grp_sem.at[9 + h], grp=to)
-
-    for h in range(2):
+    def take_all(h):
         take(h, 0, True)
-        each(groups, lambda j, h=h: take(h, j, False))
-        each(G, lambda k, h=h: send_table(k, h))
-
-    wait_all(k5.at[pl.ds(1, G - 1)], grp_sem.at[8])
+        each(groups, lambda j: take(h, j, False))
+
+        def send_table(k):
+            to = group_back(k)
+            jsend[h][k] = tacc[h][to].astype(BF)
+            send(jsend[h].at[k], jrecv[h].at[k], send_sem.at[13 + h], grp_sem.at[6 + h], grp=to)
+
+        each(G, send_table)
+
+    give_some(0, 0, groups)
+    wait_all(k1.at[pl.ds(1, G - 1)], grp_sem.at[5])
+    part = w[me_g].astype(F32)
+    for k in range(1, G):
+        part = part + k1[k].astype(F32)
+    a2[...] = jnp.zeros_like(a2)
+    for z in range(span // chunk):
+        a2[z] = part[z * chunk:(z + 1) * chunk]
+    each(Z, lambda k: send(a2.at[lax.rem(me_z + Z - k, Z)], k2.at[k], send_sem.at[16], grp_sem.at[9],
+                           shard=z_back(k)))
+    bring(1)
+    third = groups * 3 // 8
+    give_some(1, 0, third)
+    take_all(0)
+
+    wait_all(k2.at[pl.ds(1, Z - 1)], grp_sem.at[9])
+    part = a2[me_z]
+    for k in range(1, Z):
+        part = part + k2[k]
+    b3[...] = part
+    k3[0] = part
+    each(XC, lambda k: send(b3, k3.at[k], send_sem.at[17], grp_sem.at[10], shard=xc_back(k)))
+
+    give_some(1, third, 2 * third)
+    wait_all(k3.at[pl.ds(1, XC - 1)], grp_sem.at[10])
+
+    def from_xc(s):
+        dx = lax.rem(s // 2 + X - me_x, X)
+        return k3[dx * 2 + lax.rem(s % 2 + core, 2)]
+
+    part = from_xc(0)
+    for s in range(1, XC):
+        part = part + from_xc(s)
+    c4[...] = part
+    k4[0] = part
+    each(Z, lambda k: send(c4, k4.at[k], send_sem.at[18], grp_sem.at[11], shard=z_back(k)))
+
+    give_some(1, 2 * third, groups)
+    give_some(2, 0, groups)
+
+    wait_all(k4.at[pl.ds(1, Z - 1)], grp_sem.at[11])
+    for z in range(span // chunk):
+        d5[z * chunk:(z + 1) * chunk] = k4[lax.rem(z + Z - me_z, Z)].astype(BF)
+    k5[0] = d5[...]
+    each(G, lambda k: send(d5, k5.at[k], send_sem.at[19], grp_sem.at[12], grp=group_back(k)))
+
+    take_all(1)
+    take_all(2)
+
+    wait_all(k5.at[pl.ds(1, G - 1)], grp_sem.at[12])
     for g in range(G):
         total[g * span:(g + 1) * span] = k5[lax.rem(g + G - me_g, G)].astype(F32)
     lcbg_ref[...] = total[:features]
     projg_ref[...] = total[features:features + HALF]
     fmg_ref[...] = total[features + HALF:features + 2 * HALF, :width]
 
-    for h in range(2):
-        wait_all(jrecv[h].at[pl.ds(1, G - 1)], grp_sem.at[9 + h])
+    for h in range(3):
+        wait_all(jrecv[h].at[pl.ds(1, G - 1)], grp_sem.at[6 + h])
         out = tacc[h][me_g]
         for k in range(1, G):
             out = out + jrecv[h][k].astype(F32)
-        tgrad_ref[parts[h], :] = out
+        tgrad_ref[grad_parts[h], :] = out
 
     wait_all(r1.at[pl.ds(1, Z - 1)], send_sem.at[0])
     wait_all(feat_in.at[pl.ds(1, G - 1)], send_sem.at[1])
@@ -437,16 +459,16 @@
     wait_all(sbuf1.at[pl.ds(1, S - 1)], send_sem.at[4])
     wait_all(esend0.at[pl.ds(1, G - 1)], send_sem.at[5])
     wait_all(esend1.at[pl.ds(1, G - 1)], send_sem.at[6])
-    wait_all(gsend.at[pl.ds(1, G - 1)], send_sem.at[7])
-    wait_all(k1.at[pl.ds(1, G - 1)], send_sem.at[8])
-    wait_all(hsend0.at[pl.ds(1, S - 1)], send_sem.at[9])
-    wait_all(k2.at[pl.ds(1, Z - 1)], send_sem.at[10])
-    wait_all(k3.at[pl.ds(1, XC - 1)], send_sem.at[11])
-    wait_all(k4.at[pl.ds(1, Z - 1)], send_sem.at[12])
-    wait_all(hsend1.at[pl.ds(1, S - 1)], send_sem.at[13])
-    wait_all(k5.at[pl.ds(1, G - 1)], send_sem.at[14])
-    wait_all(jsend0.at[pl.ds(1, G - 1)], send_sem.at[15])
-    wait_all(jsend1.at[pl.ds(1, G - 1)], send_sem.at[16])
+    for h in range(2):
+        wait_all(gsend[h].at[pl.ds(1, G - 1)], send_sem.at[7 + h])
+    wait_all(k1.at[pl.ds(1, G - 1)], send_sem.at[9])
+    for h in range(3):
+        wait_all(hsend[h].at[pl.ds(1, S - 1)], send_sem.at[10 + h])
+        wait_all(jsend[h].at[pl.ds(1, G - 1)], send_sem.at[13 + h])
+    wait_all(k2.at[pl.ds(1, Z - 1)], send_sem.at[16])
+    wait_all(k3.at[pl.ds(1, XC - 1)], send_sem.at[17])
+    wait_all(k4.at[pl.ds(1, Z - 1)], send_sem.at[18])
+    wait_all(k5.at[pl.ds(1, G - 1)], send_sem.at[19])
 
 
 def hand_over(*refs):
@@ -474,7 +496,13 @@
     dma = pltpu.SemaphoreType.DMA
     per = rows // G
 
-    def two(shape_of, kind):
+    lead = width // 3
+    tail = width // 6
+    back_heights = (lead, width - lead)
+    grad_heights = (lead, width - lead - tail, tail)
+    span = (features + 2 * HALF) // G
+
+    def two(shape_of, kind, heights=heights):
         return [vm(shape_of(height), kind) for height in heights]
 
     scratch = [
@@ -494,30 +522,30 @@
         *two(lambda m: (G, m * 3 // 4, LANES), BF),
         *two(lambda m: (G, m * 3 // 4, LANES), BF),
         vm((2 * features, G * LANES), BF),
-        vm((G, width * 3 // 4, LANES), BF),
-        vm((G, width * 3 // 4, LANES), BF),
+        *two(lambda m: (G, m * 3 // 4, LANES), BF, back_heights),
+        *two(lambda m: (G, m * 3 // 4, LANES), BF, back_heights),
         vm((width, bag_lanes), BF),
-        *two(lambda m: (S, m // 2, LANES), BF),
-        *two(lambda m: (S, m // 2, LANES), BF),
-        *two(lambda m: (G, m, per), F32),
-        *two(lambda m: (G, m, per), BF),
-        *two(lambda m: (G, m, per), BF),
-        vm((G, Z * chunk, features), BF),
-        vm((G, Z * chunk, features), BF),
+        *two(lambda m: (S, m // 2, LANES), BF, grad_heights),
+        *two(lambda m: (S, m // 2, LANES), BF, grad_heights),
+        *two(lambda m: (G, m, per), F32, grad_heights),
+        *two(lambda m: (G, m, per), BF, grad_heights),
+        *two(lambda m: (G, m, per), BF, grad_heights),
+        vm((G, span, features), BF),
+        vm((G, span, features), BF),
         vm((Z, chunk, features), F32),
         vm((Z, chunk, features), F32),
         vm((chunk, features), F32),
         vm((XC, chunk, features), F32),
         vm((chunk, features), F32),
         vm((Z, chunk, features), F32),
-        vm((Z * chunk, features), BF),
-        vm((G, Z * chunk, features), BF),
-        vm((G * Z * chunk, features), F32),
-        dma((17,)),
-        dma((2,)),
+        vm((span, features), BF),
+        vm((G, span, features), BF),
+        vm((G * span, features), F32),
+        dma((20,)),
+        dma((groups,)),
         dma((2 * groups,)),
-        dma((2 * groups,)),
-        dma((11,)),
+        dma((3 * groups,)),
+        dma((13,)),
     ]
     whole = pl.BlockSpec(memory_space=pltpu.VMEM)
     shapes = (

time: 136 us -> 128 us (0.941)
  Pallas kernels: 136 us -> 127 us
    pallas_call x1, Pallas kernels: 134 us -> 125 us  [shards(): pl.pallas_call(functools.partial(kernel, X, Z, G), out_shape=shapes, in_s...]
where the time goes in v3:
time: 128 us
  Pallas kernels  127 us (99%)
    pallas_call x1, Pallas kernels, shards(): pl.pallas_call(functools.partial(kernel, X, Z, G), out_shape=shapes, in_s...  125 us

profile of v3, /device:TPU:1, one launch (start us, length us, event | category | flops | bytes accessed | tf_op | source)
XLA Modules:
  0.0 127.9 jit_solution(3788468671163859604)
XLA Ops:
  0.6 125.2 %shard_map.128 = (bf16[2,192,256]{2,1,0:T(8,128)(2,1)}, f32[192,256]{1,0:T(8,128)}, f32[256,256]{1,0:T(8,128)}, f32[64,256]{1,0:T(8,128)}, f32[64,192]{1,0:T(8,128)}) custom-call(s32[64,64]{1,0:T(8,128)} %bitcast.11, s32[16,4,48]{2,1,0:T(4,128)} %bitcast.12, s32[1,48]{1,0:T(1,128)} %feat_ref.1, bf16[192,2048]{1,0:T(8,128)(2,1)} %bitcast.9, ...), custom_call_target="tpu_custom_call" | custom-call | tf_op jit(solution)/shard_map/pallas_call | solution.py:558
  125.9 2.1 %shard_map.129 = (bf16[2,192,256]{2,1,0:T(8,128)(2,1)}, f32[192,256]{1,0:T(8,128)}, f32[256,256]{1,0:T(8,128)}, f32[64,256]{1,0:T(8,128)}, f32[64,192]{1,0:T(8,128)}) custom-call(bf16[2,192,256]{2,1,0:T(8,128)(2,1)} %get-tuple-element.15.refs_0_, f32[192,256]{1,0:T(8,128)} %get-tuple-element.16.refs_1_, f32[256,256]{1,0:T(8,128)} %get-tuple-element.17.refs_2_, ...), custom_call_target="tpu_custom_call" | custom-call | tf_op jit(solution)/shard_map/pallas_call | solution.py:571

commit v4 on v3

--- a/solution.py
+++ b/solution.py
@@ -69,7 +69,7 @@
     sbuf0, sbuf1, rbuf0, rbuf1, wide0, wide1, pooled0, pooled1, esend0, esend1, erecv0, erecv1,
     pm, gsend0, gsend1, grecv0, grecv1, gt, hsend0, hsend1, hsend2, hrecv0, hrecv1, hrecv2,
     tacc0, tacc1, tacc2, jsend0, jsend1, jsend2, jrecv0, jrecv1, jrecv2,
-    w, k1, a2, k2, b3, k3, c4, k4, d5, k5, total,
+    w, k1, a2, k2, b3, k3, c4, k4, total,
     send_sem, list_sem, row_sem, grad_sem, grp_sem,
 ):
     S = X * Z * 2
@@ -325,15 +325,16 @@
         fm_grad = fm_grad + nt(crossed_t, grad_low)
         proj_grad = proj_grad + nn(grad_proj_t, xt)
         lcb_grad = lcb_grad + nn(x, grad_low)
-    chunk = a2.shape[1]
     span = w.shape[1]
-    total[...] = jnp.zeros_like(total)
     total[:features] = lcb_grad
     total[features:features + HALF] = proj_grad
-    total[features + HALF:features + 2 * HALF, :width] = fm_grad
-    for g in range(G):
-        w[g] = total[g * span:(g + 1) * span].astype(BF)
-    each(G, lambda k: send(w.at[group_back(k)], k1.at[k], send_sem.at[9], grp_sem.at[5], grp=group_back(k)))
+    total[features + HALF:features + 2 * HALF, :] = jnp.concatenate(
+        [fm_grad, jnp.zeros((fm.shape[0], total.shape[1] - width), F32)], axis=1
+    ) if total.shape[1] > width else fm_grad
+    for z in range(Z):
+        w[z] = total[z * span:(z + 1) * span].astype(BF)
+    each(Z, lambda k: send(w.at[lax.rem(me_z + Z - k, Z)], k1.at[k], send_sem.at[9], grp_sem.at[5],
+                           shard=z_back(k)))
     send_back(1)
 
     def bring(h):
@@ -390,57 +391,44 @@
         each(G, send_table)
 
     give_some(0, 0, groups)
-    wait_all(k1.at[pl.ds(1, G - 1)], grp_sem.at[5])
-    part = w[me_g].astype(F32)
-    for k in range(1, G):
+    wait_all(k1.at[pl.ds(1, Z - 1)], grp_sem.at[5])
+    part = w[me_z].astype(F32)
+    for k in range(1, Z):
         part = part + k1[k].astype(F32)
-    a2[...] = jnp.zeros_like(a2)
-    for z in range(span // chunk):
-        a2[z] = part[z * chunk:(z + 1) * chunk]
-    each(Z, lambda k: send(a2.at[lax.rem(me_z + Z - k, Z)], k2.at[k], send_sem.at[16], grp_sem.at[9],
-                           shard=z_back(k)))
+    a2[...] = part.astype(BF)
+    k2[0] = a2[...]
+    each(G, lambda k: send(a2, k2.at[k], send_sem.at[16], grp_sem.at[9], grp=group_back(k)))
+
     bring(1)
-    third = groups * 3 // 8
-    give_some(1, 0, third)
+    give_some(1, 0, groups)
+    wait_all(k2.at[pl.ds(1, G - 1)], grp_sem.at[9])
+    part = k2[lax.rem(G - me_g, G)].astype(F32)
+    for g in range(1, G):
+        part = part + k2[lax.rem(g + G - me_g, G)].astype(F32)
+    b3[...] = part.astype(BF)
+    k3[0] = b3[...]
+    each(XC, lambda k: send(b3, k3.at[k], send_sem.at[17], grp_sem.at[10], shard=xc_back(k)))
+
     take_all(0)
-
-    wait_all(k2.at[pl.ds(1, Z - 1)], grp_sem.at[9])
-    part = a2[me_z]
-    for k in range(1, Z):
-        part = part + k2[k]
-    b3[...] = part
-    k3[0] = part
-    each(XC, lambda k: send(b3, k3.at[k], send_sem.at[17], grp_sem.at[10], shard=xc_back(k)))
-
-    give_some(1, third, 2 * third)
+    give_some(2, 0, groups)
+    take_all(1)
     wait_all(k3.at[pl.ds(1, XC - 1)], grp_sem.at[10])
 
     def from_xc(s):
         dx = lax.rem(s // 2 + X - me_x, X)
-        return k3[dx * 2 + lax.rem(s % 2 + core, 2)]
+        return k3[dx * 2 + lax.rem(s % 2 + core, 2)].astype(F32)
 
     part = from_xc(0)
     for s in range(1, XC):
         part = part + from_xc(s)
-    c4[...] = part
-    k4[0] = part
+    c4[...] = part.astype(BF)
+    k4[0] = c4[...]
     each(Z, lambda k: send(c4, k4.at[k], send_sem.at[18], grp_sem.at[11], shard=z_back(k)))
-
-    give_some(1, 2 * third, groups)
-    give_some(2, 0, groups)
+    take_all(2)
 
     wait_all(k4.at[pl.ds(1, Z - 1)], grp_sem.at[11])
-    for z in range(span // chunk):
-        d5[z * chunk:(z + 1) * chunk] = k4[lax.rem(z + Z - me_z, Z)].astype(BF)
-    k5[0] = d5[...]
-    each(G, lambda k: send(d5, k5.at[k], send_sem.at[19], grp_sem.at[12], grp=group_back(k)))
-
-    take_all(1)
-    take_all(2)
-
-    wait_all(k5.at[pl.ds(1, G - 1)], grp_sem.at[12])
-    for g in range(G):
-        total[g * span:(g + 1) * span] = k5[lax.rem(g + G - me_g, G)].astype(F32)
+    for z in range(Z):
+        total[z * span:(z + 1) * span] = k4[lax.rem(z + Z - me_z, Z)].astype(F32)
     lcbg_ref[...] = total[:features]
     projg_ref[...] = total[features:features + HALF]
     fmg_ref[...] = total[features + HALF:features + 2 * HALF, :width]
@@ -461,14 +449,13 @@
     wait_all(esend1.at[pl.ds(1, G - 1)], send_sem.at[6])
     for h in range(2):
         wait_all(gsend[h].at[pl.ds(1, G - 1)], send_sem.at[7 + h])
-    wait_all(k1.at[pl.ds(1, G - 1)], send_sem.at[9])
+    wait_all(k1.at[pl.ds(1, Z - 1)], send_sem.at[9])
     for h in range(3):
         wait_all(hsend[h].at[pl.ds(1, S - 1)], send_sem.at[10 + h])
         wait_all(jsend[h].at[pl.ds(1, G - 1)], send_sem.at[13 + h])
-    wait_all(k2.at[pl.ds(1, Z - 1)], send_sem.at[16])
+    wait_all(k2.at[pl.ds(1, G - 1)], send_sem.at[16])
     wait_all(k3.at[pl.ds(1, XC - 1)], send_sem.at[17])
     wait_all(k4.at[pl.ds(1, Z - 1)], send_sem.at[18])
-    wait_all(k5.at[pl.ds(1, G - 1)], send_sem.at[19])
 
 
 def hand_over(*refs):
@@ -489,7 +476,6 @@
     rank = proj_weight.shape[1]
     groups = X * 2
     bag_lanes = samples // 2 * LANES
-    chunk = -(-(features + 2 * HALF) // (G * Z * 8)) * 8
     cut = width * 2 // 3
     heights = (cut, width - cut)
     vm = pltpu.VMEM
@@ -497,10 +483,9 @@
     per = rows // G
 
     lead = width // 3
-    tail = width // 6
     back_heights = (lead, width - lead)
-    grad_heights = (lead, width - lead - tail, tail)
-    span = (features + 2 * HALF) // G
+    grad_heights = (lead, lead, width - 2 * lead)
+    span = (features + 2 * HALF) // Z
 
     def two(shape_of, kind, heights=heights):
         return [vm(shape_of(height), kind) for height in heights]
@@ -530,22 +515,20 @@
         *two(lambda m: (G, m, per), F32, grad_heights),
         *two(lambda m: (G, m, per), BF, grad_heights),
         *two(lambda m: (G, m, per), BF, grad_heights),
-        vm((G, span, features), BF),
-        vm((G, span, features), BF),
-        vm((Z, chunk, features), F32),
-        vm((Z, chunk, features), F32),
-        vm((chunk, features), F32),
-        vm((XC, chunk, features), F32),
-        vm((chunk, features), F32),
-        vm((Z, chunk, features), F32),
+        vm((Z, span, features), BF),
+        vm((Z, span, features), BF),
         vm((span, features), BF),
         vm((G, span, features), BF),
-        vm((G * span, features), F32),
-        dma((20,)),
+        vm((span, features), BF),
+        vm((XC, span, features), BF),
+        vm((span, features), BF),
+        vm((Z, span, features), BF),
+        vm((Z * span, features), F32),
+        dma((19,)),
         dma((groups,)),
         dma((2 * groups,)),
         dma((3 * groups,)),
-        dma((13,)),
+        dma((12,)),
     ]
     whole = pl.BlockSpec(memory_space=pltpu.VMEM)
     shapes = (

time: 128 us -> 125 us (0.977)
  Pallas kernels: 127 us -> 124 us
    pallas_call x1, Pallas kernels: 125 us -> 122 us  [shards(): pl.pallas_call(functools.partial(kernel, X, Z, G), out_shape=shapes, in_s...]
where the time goes in v4:
time: 125 us; the launch traced here: 124 us
  Pallas kernels  124 us (99%)
    pallas_call x1, Pallas kernels, shards(): pl.pallas_call(functools.partial(kernel, X, Z, G), out_shape=shapes, in_s...  122 us

profile of v4, /device:TPU:1, one launch (start us, length us, event | category | flops | bytes accessed | tf_op | source)
XLA Modules:
  0.0 124.4 jit_solution(5362587295016697251)
XLA Ops:
  0.6 121.7 %shard_map.128 = (bf16[2,192,256]{2,1,0:T(8,128)(2,1)}, f32[192,256]{1,0:T(8,128)}, f32[256,256]{1,0:T(8,128)}, f32[64,256]{1,0:T(8,128)}, f32[64,192]{1,0:T(8,128)}) custom-call(s32[64,64]{1,0:T(8,128)} %bitcast.11, s32[16,4,48]{2,1,0:T(4,128)} %bitcast.12, s32[1,48]{1,0:T(1,128)} %feat_ref.1, bf16[192,2048]{1,0:T(8,128)(2,1)} %bitcast.9, ...), custom_call_target="tpu_custom_call" | custom-call | tf_op jit(solution)/shard_map/pallas_call | solution.py:541
  122.3 2.1 %shard_map.129 = (bf16[2,192,256]{2,1,0:T(8,128)(2,1)}, f32[192,256]{1,0:T(8,128)}, f32[256,256]{1,0:T(8,128)}, f32[64,256]{1,0:T(8,128)}, f32[64,192]{1,0:T(8,128)}) custom-call(bf16[2,192,256]{2,1,0:T(8,128)(2,1)} %get-tuple-element.15.refs_0_, f32[192,256]{1,0:T(8,128)} %get-tuple-element.16.refs_1_, f32[256,256]{1,0:T(8,128)} %get-tuple-element.17.refs_2_, ...), custom_call_target="tpu_custom_call" | custom-call | tf_op jit(solution)/shard_map/pallas_call | solution.py:554

commit v5 on v4

--- a/solution.py
+++ b/solution.py
@@ -63,14 +63,15 @@
 
 def kernel(
     X, Z, G,
-    lists_ref, bag_ref, feat_ref, table_ref, lcb_ref, projt_ref, fm_ref, gain_ref, cot_ref,
+    lists_ref, bag_ref, feat_ref, table_far, lcb_far, projt_far, fm_ref, gain_ref, cot_far,
     inter_ref, tgrad_ref, lcbg_ref, projg_ref, fmg_ref,
     l1, r1, r1t, r2, bagl, feat_own, feat_in, oh, mt,
     sbuf0, sbuf1, rbuf0, rbuf1, wide0, wide1, pooled0, pooled1, esend0, esend1, erecv0, erecv1,
-    pm, gsend0, gsend1, grecv0, grecv1, gt, hsend0, hsend1, hsend2, hrecv0, hrecv1, hrecv2,
-    tacc0, tacc1, tacc2, jsend0, jsend1, jsend2, jrecv0, jrecv1, jrecv2,
+    pm, gsend0, gsend1, grecv0, grecv1, gt, hsend0, hsend1, hsend2, hsend3, hrecv0, hrecv1, hrecv2, hrecv3,
+    tacc0, tacc1, tacc2, tacc3, jsend0, jsend1, jsend2, jsend3, jrecv0, jrecv1, jrecv2, jrecv3,
     w, k1, a2, k2, b3, k3, c4, k4, total,
-    send_sem, list_sem, row_sem, grad_sem, grp_sem,
+    table_ref, lcb_ref, projt_ref, cot_ref,
+    send_sem, list_sem, row_sem, grad_sem, grp_sem, stage_sem,
 ):
     S = X * Z * 2
     XC = X * 2
@@ -89,12 +90,14 @@
     sbuf, rbuf, wide, pooled = (sbuf0, sbuf1), (rbuf0, rbuf1), (wide0, wide1), (pooled0, pooled1)
     esend, erecv = (esend0, esend1), (erecv0, erecv1)
     gsend, grecv = (gsend0, gsend1), (grecv0, grecv1)
-    hsend, hrecv, tacc = (hsend0, hsend1, hsend2), (hrecv0, hrecv1, hrecv2), (tacc0, tacc1, tacc2)
-    jsend, jrecv = (jsend0, jsend1, jsend2), (jrecv0, jrecv1, jrecv2)
+    hsend, hrecv = (hsend0, hsend1, hsend2, hsend3), (hrecv0, hrecv1, hrecv2, hrecv3)
+    tacc = (tacc0, tacc1, tacc2, tacc3)
+    jsend, jrecv = (jsend0, jsend1, jsend2, jsend3), (jrecv0, jrecv1, jrecv2, jrecv3)
     lead = tacc0.shape[1]
     mid = lead + tacc1.shape[1]
+    last = mid + tacc2.shape[1]
     back_parts = (slice(0, lead), slice(lead, width))
-    grad_parts = (slice(0, lead), slice(lead, mid), slice(mid, width))
+    grad_parts = (slice(0, lead), slice(lead, mid), slice(mid, last), slice(last, width))
     cut = wide0.shape[0]
     parts = (slice(0, cut), slice(cut, width))
 
@@ -138,6 +141,13 @@
 
         lax.fori_loop(first, count, step, 0)
 
+    def mixed(q):
+        return lax.div(q, Z) * Z + lax.rem(lax.rem(q, Z) * 3, Z)
+
+    def across(q, src, dst, ssem, rsem, base, back):
+        at = mixed(q)
+        send(src.at[at], dst.at[at], ssem, rsem.at[base + lax.div(q, Z)], shard=peer(at, back))
+
     barrier = pltpu.get_barrier_semaphore()
 
     def greet(**where):
@@ -146,6 +156,15 @@
     each(Z, lambda k: greet(shard=z_back(k)))
     each(XC, lambda k: greet(shard=xc_back(k)))
     each(G, lambda k: greet(grp=group_back(k)))
+
+    staged = [
+        pltpu.make_async_copy(far, near, stage_sem.at[i])
+        for i, (far, near) in enumerate((
+            (table_far, table_ref), (lcb_far, lcb_ref), (projt_far, projt_ref), (cot_far, cot_ref)
+        ))
+    ]
+    for copy in staged:
+        copy.start()
 
     lists = jnp.concatenate([lists_ref[...], lists_ref[...]], axis=1)
     for z in range(Z):
@@ -200,16 +219,18 @@
                 sbuf[h][j * Z + 2 * p] = even
                 sbuf[h][j * Z + 2 * p + 1] = odd
 
-        each(j * Z + Z, lambda q: send(sbuf0.at[q], rbuf0.at[q], send_sem.at[3], row_sem.at[j],
-                                       shard=peer(q, False)),
+        each(j * Z + Z, lambda q: across(q, sbuf0, rbuf0, send_sem.at[3], row_sem, 0, False),
              first=j * Z + (1 if first else 0))
 
+    staged[0].wait()
     serve(0, True)
     each(groups, lambda j: serve(j, False))
-    each(S, lambda q: send(sbuf1.at[q], rbuf1.at[q], send_sem.at[4], row_sem.at[groups + lax.div(q, Z)],
-                           shard=peer(q, False)))
+    each(S, lambda q: across(q, sbuf1, rbuf1, send_sem.at[4], row_sem, groups, False))
     for h in range(2):
         rbuf[h][0] = sbuf[h][0]
+
+    for copy in staged[1:]:
+        copy.wait()
 
     bagl[...] = jnp.full(bagl.shape, -1, jnp.int32)
     for n in range(samples):
@@ -268,13 +289,15 @@
         each(G, lambda k, h=h: send(esend[h].at[k], erecv[h].at[k], send_sem.at[5 + h], grp_sem.at[1 + h],
                                     grp=group_back(k)))
         erecv[h][0] = esend[h][0]
+    arrived = []
+    both = []
     for h in range(2):
         wait_all(erecv[h].at[pl.ds(1, G - 1)], grp_sem.at[1 + h])
-
-    arrived = jnp.concatenate([
-        jnp.concatenate([unpack_dense(erecv[h][k], lane) for h in range(2)], axis=0) for k in range(G)
-    ], axis=1)
-    both = nt(arrived, pm[...]).astype(BF)
+        arrived.append(jnp.concatenate([unpack_dense(erecv[h][k], lane) for k in range(G)], axis=1))
+        both.append(nt(arrived[h], pm[...]).astype(BF))
+
+    arrived = jnp.concatenate(arrived, axis=0)
+    both = jnp.concatenate(both, axis=0)
     lcb = lcb_ref[...]
     projt = projt_ref[...]
     grads_in = []
@@ -345,15 +368,18 @@
     bring(0)
 
     def give(h, j, first):
-        slot_grad = nt(gt[grad_parts[h], :], mt[j])
-        for p in range(Z // 2):
-            even, odd = pack_pair(slot_grad[:, p * LANES:(p + 1) * LANES], low)
-            hsend[h][j * Z + 2 * p] = even
-            hsend[h][j * Z + 2 * p + 1] = odd
-        if first:
-            hrecv[h][0] = hsend[h][0]
-        each(j * Z + Z, lambda q: send(hsend[h].at[q], hrecv[h].at[q], send_sem.at[10 + h],
-                                       grad_sem.at[h * groups + j], shard=peer(q, True)),
+        made = (0,) if h == 0 else (1, 2, 3)
+        low_row, high_row = grad_parts[made[0]].start, grad_parts[made[-1]].stop
+        slot_grad = nt(gt[low_row:high_row, :], mt[j])
+        for to in made:
+            part = slot_grad[grad_parts[to].start - low_row:grad_parts[to].stop - low_row]
+            for p in range(Z // 2):
+                even, odd = pack_pair(part[:, p * LANES:(p + 1) * LANES], low)
+                hsend[to][j * Z + 2 * p] = even
+                hsend[to][j * Z + 2 * p + 1] = odd
+            if first:
+                hrecv[to][0] = hsend[to][0]
+        each(j * Z + Z, lambda q: across(q, hsend[h], hrecv[h], send_sem.at[10 + h], grad_sem, h * groups, True),
              first=j * Z + (1 if first else 0))
 
     def give_some(h, first, last):
@@ -386,7 +412,7 @@
         def send_table(k):
             to = group_back(k)
             jsend[h][k] = tacc[h][to].astype(BF)
-            send(jsend[h].at[k], jrecv[h].at[k], send_sem.at[13 + h], grp_sem.at[6 + h], grp=to)
+            send(jsend[h].at[k], jrecv[h].at[k], send_sem.at[14 + h], grp_sem.at[6 + h], grp=to)
 
         each(G, send_table)
 
@@ -397,22 +423,24 @@
         part = part + k1[k].astype(F32)
     a2[...] = part.astype(BF)
     k2[0] = a2[...]
-    each(G, lambda k: send(a2, k2.at[k], send_sem.at[16], grp_sem.at[9], grp=group_back(k)))
+    each(G, lambda k: send(a2, k2.at[k], send_sem.at[18], grp_sem.at[10], grp=group_back(k)))
 
     bring(1)
     give_some(1, 0, groups)
-    wait_all(k2.at[pl.ds(1, G - 1)], grp_sem.at[9])
+    wait_all(k2.at[pl.ds(1, G - 1)], grp_sem.at[10])
     part = k2[lax.rem(G - me_g, G)].astype(F32)
     for g in range(1, G):
         part = part + k2[lax.rem(g + G - me_g, G)].astype(F32)
     b3[...] = part.astype(BF)
     k3[0] = b3[...]
-    each(XC, lambda k: send(b3, k3.at[k], send_sem.at[17], grp_sem.at[10], shard=xc_back(k)))
+    each(XC, lambda k: send(b3, k3.at[k], send_sem.at[19], grp_sem.at[11], shard=xc_back(k)))
+
+    for h in (2, 3):
+        each(S, lambda q, h=h: across(q, hsend[h], hrecv[h], send_sem.at[10 + h], grad_sem, h * groups, True))
 
     take_all(0)
-    give_some(2, 0, groups)
     take_all(1)
-    wait_all(k3.at[pl.ds(1, XC - 1)], grp_sem.at[10])
+    wait_all(k3.at[pl.ds(1, XC - 1)], grp_sem.at[11])
 
     def from_xc(s):
         dx = lax.rem(s // 2 + X - me_x, X)
@@ -423,17 +451,18 @@
         part = part + from_xc(s)
     c4[...] = part.astype(BF)
     k4[0] = c4[...]
-    each(Z, lambda k: send(c4, k4.at[k], send_sem.at[18], grp_sem.at[11], shard=z_back(k)))
+    each(Z, lambda k: send(c4, k4.at[k], send_sem.at[20], grp_sem.at[12], shard=z_back(k)))
     take_all(2)
-
-    wait_all(k4.at[pl.ds(1, Z - 1)], grp_sem.at[11])
+    take_all(3)
+
+    wait_all(k4.at[pl.ds(1, Z - 1)], grp_sem.at[12])
     for z in range(Z):
         total[z * span:(z + 1) * span] = k4[lax.rem(z + Z - me_z, Z)].astype(F32)
     lcbg_ref[...] = total[:features]
     projg_ref[...] = total[features:features + HALF]
     fmg_ref[...] = total[features + HALF:features + 2 * HALF, :width]
 
-    for h in range(3):
+    for h in range(4):
         wait_all(jrecv[h].at[pl.ds(1, G - 1)], grp_sem.at[6 + h])
         out = tacc[h][me_g]
         for k in range(1, G):
@@ -450,18 +479,22 @@
     for h in range(2):
         wait_all(gsend[h].at[pl.ds(1, G - 1)], send_sem.at[7 + h])
     wait_all(k1.at[pl.ds(1, Z - 1)], send_sem.at[9])
-    for h in range(3):
+    for h in range(4):
         wait_all(hsend[h].at[pl.ds(1, S - 1)], send_sem.at[10 + h])
-        wait_all(jsend[h].at[pl.ds(1, G - 1)], send_sem.at[13 + h])
-    wait_all(k2.at[pl.ds(1, G - 1)], send_sem.at[16])
-    wait_all(k3.at[pl.ds(1, XC - 1)], send_sem.at[17])
-    wait_all(k4.at[pl.ds(1, Z - 1)], send_sem.at[18])
+        wait_all(jsend[h].at[pl.ds(1, G - 1)], send_sem.at[14 + h])
+    wait_all(k2.at[pl.ds(1, G - 1)], send_sem.at[18])
+    wait_all(k3.at[pl.ds(1, XC - 1)], send_sem.at[19])
+    wait_all(k4.at[pl.ds(1, Z - 1)], send_sem.at[20])
 
 
 def hand_over(*refs):
     half = len(refs) // 2
-    for i in range(half):
-        refs[half + i][...] = refs[i][...]
+    sems = refs[-1]
+    copies = [pltpu.make_async_copy(refs[i], refs[half + i], sems.at[i]) for i in range(half)]
+    for copy in copies:
+        copy.start()
+    for copy in copies:
+        copy.wait()
 
 
 def shards(X, Z, emb_table, touched, bag_slots, feat_of_slot, lcb_weight, proj_weight, fm_weight,
@@ -484,7 +517,8 @@
 
     lead = width // 3
     back_heights = (lead, width - lead)
-    grad_heights = (lead, lead, width - 2 * lead)
+    tail = lead // 2
+    grad_heights = (lead, lead, tail, width - 2 * lead - tail)
     span = (features + 2 * HALF) // Z
 
     def two(shape_of, kind, heights=heights):
@@ -524,13 +558,19 @@
         vm((span, features), BF),
         vm((Z, span, features), BF),
         vm((Z * span, features), F32),
-        dma((19,)),
+        vm(table_t.shape, BF),
+        vm(lcb_weight.shape, BF),
+        vm((rank, features), BF),
+        vm((2, width, features), BF),
+        dma((21,)),
         dma((groups,)),
         dma((2 * groups,)),
-        dma((3 * groups,)),
-        dma((12,)),
+        dma((4 * groups,)),
+        dma((13,)),
+        dma((4,)),
     ]
     whole = pl.BlockSpec(memory_space=pltpu.VMEM)
+    far = pl.BlockSpec(memory_space=pl.ANY)
     shapes = (
         jax.ShapeDtypeStruct((2, width, features), BF),
         jax.ShapeDtypeStruct((width, per), F32),
@@ -541,7 +581,7 @@
     results = pl.pallas_call(
         functools.partial(kernel, X, Z, G),
         out_shape=shapes,
-        in_specs=[whole] * 9,
+        in_specs=[whole, whole, whole, far, far, far, whole, whole, far],
         out_specs=[whole] * 5,
         scratch_shapes=scratch,
         compiler_params=pltpu.CompilerParams(
@@ -554,8 +594,9 @@
     inter, tgrad, lcbg, projg, fmg = pl.pallas_call(
         hand_over,
         out_shape=shapes,
-        in_specs=[whole] * 5,
+        in_specs=[far] * 5,
         out_specs=[whole] * 5,
+        scratch_shapes=[dma((5,))],
     )(*results)
     return (jnp.transpose(inter, (0, 2, 1)), tgrad.T, lcbg, projg.T, fmg)
 

time: 125 us -> 123 us (0.984)
  Pallas kernels: 124 us -> 122 us
    pallas_call x1, Pallas kernels: 122 us -> 120 us  [shards(): pl.pallas_call(functools.partial(kernel, X, Z, G), out_shape=shapes, in_s...]
where the time goes in v5:
time: 123 us; the launch traced here: 122 us
  Pallas kernels  122 us (99%)
    pallas_call x1, Pallas kernels, shards(): pl.pallas_call(functools.partial(kernel, X, Z, G), out_shape=shapes, in_s...  120 us

profile of v5, /device:TPU:1, one launch (start us, length us, event | category | flops | bytes accessed | tf_op | source)
XLA Modules:
  0.0 122.4 jit_solution(3942223491907129313)
XLA Ops:
  0.6 119.7 %shard_map.128 = (bf16[2,192,256]{2,1,0:T(8,128)(2,1)}, f32[192,256]{1,0:T(8,128)}, f32[256,256]{1,0:T(8,128)}, f32[64,256]{1,0:T(8,128)}, f32[64,192]{1,0:T(8,128)}) custom-call(s32[64,64]{1,0:T(8,128)} %bitcast.11, s32[16,4,48]{2,1,0:T(4,128)} %bitcast.12, s32[1,48]{1,0:T(1,128)} %feat_ref.1, bf16[192,2048]{1,0:T(8,128)(2,1)} %bitcast.9, ...), custom_call_target="tpu_custom_call" | custom-call | tf_op jit(solution)/shard_map/pallas_call | solution.py:581
  120.4 2.1 %shard_map.129 = (bf16[2,192,256]{2,1,0:T(8,128)(2,1)}, f32[192,256]{1,0:T(8,128)}, f32[256,256]{1,0:T(8,128)}, f32[64,256]{1,0:T(8,128)}, f32[64,192]{1,0:T(8,128)}) custom-call(bf16[2,192,256]{2,1,0:T(8,128)(2,1)} %get-tuple-element.15.refs_0_, f32[192,256]{1,0:T(8,128)} %get-tuple-element.16.refs_1_, f32[256,256]{1,0:T(8,128)} %get-tuple-element.17.refs_2_, ...), custom_call_target="tpu_custom_call" | custom-call | tf_op jit(solution)/shard_map/pallas_call | solution.py:594
